TPU v7x, 256 devices: a whole 4x4x8 slice. The times are simulated.
256 devices in a mesh: row: 8 (over y, core), col: 32 (over x, z).
Axes of the slice: x: 4, y: 4, z: 8, core: 2. Of those that a mesh axis runs over, the one named last changes fastest.
Arguments:
- radial: bfloat16 [640, 48, 1024], P('col', None, 'row'), may hold values from -1 to 1
- form_factors: float32 [256, 1024], replicated, may hold values from -6 to 6
- coupling: int32 [320, 640], P('row', 'col'), may hold values from 0 to 15
- quantum: int32 [640, 3], replicated, may hold values from 0 to 3
- green_diag: float32 [640, 48], P('col'), may hold values from -0.1 to 0.1
- kmatrix: bfloat16 [30720, 128], P('col'), may hold values from -6 to 6
- born_term: float32 [15360, 128], P('row'), may hold values from -3 to 3
Outputs:
- v_block: bfloat16 [15360, 30720], P('row', 'col')
- first_iterate: bfloat16 [15360, 128], P('row')
- second_iterate: float32 [15360, 128], P('row', 'col')
All inputs are finite; a program needn't handle non-finite values.
Results may differ from a plain program's by a relative error of at most 0.008.
Values may be sent and summed in bfloat16 or wider, within the bound.
A program may use at most 128 MiB of HBM per device.

v0:
```python
import math

import jax
import jax.numpy as jnp
from jax import lax
from jax.sharding import PartitionSpec as P

NTARG = 4


def broadcast(value, axis, source):
    kept = jnp.where(lax.axis_index(axis) == source, value, 0).astype(value.dtype)
    return lax.psum(kept, axis)


def body(radial, form_factors, coupling, quantum, green_diag, kmatrix, born_term):
    col_panel = lax.all_gather(radial, "row", axis=2, tiled=True)
    col_count = col_panel.shape[0]
    mom_count = col_panel.shape[1]
    grid_count = col_panel.shape[2]
    row_count = coupling.shape[0]
    row_size = lax.axis_size("row")
    row_index = lax.axis_index("row")
    col_index = lax.axis_index("col")
    slab_total = row_count * row_size
    call_count = max(1, row_count // col_count)
    first_owner = row_index * row_count // col_count
    owner_panels = []
    for member in range(call_count):
        owner_panels.append(broadcast(col_panel, "col", first_owner + member))
    joined = jnp.concatenate(owner_panels, axis=0)
    row_quant = lax.dynamic_slice_in_dim(quantum, row_index * row_count, row_count, 0)
    col_quant = lax.dynamic_slice_in_dim(quantum, col_index * col_count, col_count, 0)
    table_index = coupling * (NTARG * NTARG) + row_quant[:, 2:3] * NTARG + col_quant[:, 2][None, :]
    parity = (row_quant[:, 0:1] + col_quant[:, 0][None, :]) % 2
    spread_m = jnp.abs(row_quant[:, 1:2] - col_quant[:, 1][None, :])
    angular = (1.0 - 2.0 * parity.astype(jnp.float32)) / (1.0 + spread_m.astype(jnp.float32))
    weights = jnp.take(form_factors, table_index, axis=0) * angular[:, :, None]
    group_size = math.gcd(row_count, 5)

    def build_rows(operands):
        panel_rows, weight_rows = operands
        scaled = (weight_rows[:, :, None, :] * col_panel[None, :, :, :]).astype(jnp.bfloat16)
        scaled = scaled.reshape(group_size, col_count * mom_count, grid_count)
        return jnp.einsum(
            "akr,anr->akn", panel_rows, scaled, preferred_element_type=jnp.float32
        ).astype(jnp.bfloat16)

    blocks = lax.map(
        build_rows,
        (
            joined.reshape(row_count // group_size, group_size, mom_count, grid_count),
            weights.reshape(row_count // group_size, group_size, col_count, grid_count),
        ),
    )
    v_block = blocks.reshape(row_count * mom_count, col_count * mom_count)
    green_flat = green_diag.reshape(-1, 1)
    weighted = (green_flat * kmatrix).astype(jnp.bfloat16)
    partial_value = jnp.dot(v_block, weighted, preferred_element_type=jnp.float32)
    summed = lax.psum(partial_value, "col")
    first_iterate = (born_term + summed).astype(jnp.bfloat16)
    block_rows = col_count * mom_count
    in_slab = col_index * col_count < slab_total
    gathered = lax.all_gather(first_iterate, "row", axis=0, tiled=True)
    start_row = jnp.minimum(col_index * block_rows, slab_total * mom_count - block_rows)
    fresh_rows = lax.dynamic_slice_in_dim(gathered, start_row, block_rows, 0)
    updated = jnp.where(in_slab, fresh_rows, kmatrix)
    weighted_next = (green_flat * updated).astype(jnp.bfloat16)
    partial_next = jnp.dot(v_block, weighted_next, preferred_element_type=jnp.float32)
    col_share = lax.psum_scatter(partial_next, "col", scatter_dimension=1, tiled=True)
    share_width = col_share.shape[1]
    born_share = lax.dynamic_slice_in_dim(born_term, col_index * share_width, share_width, 1)
    second_iterate = born_share + col_share
    return (v_block, first_iterate, second_iterate)


def solution(mesh):
    placed = (
        P("col", None, "row"),
        P(),
        P("row", "col"),
        P(),
        P("col", None),
        P("col", None),
        P("row", None),
    )
    return jax.shard_map(
        body,
        mesh=mesh,
        in_specs=placed,
        out_specs=(P("row", "col"), P("row", None), P("row", "col")),
        check_vma=False,
    )
```

profile of v0, /device:TPU:1, one launch (start us, length us, event | category | flops | bytes accessed | tf_op | source)
XLA Modules:
  0.0 713.5 jit_solution(1969080752359719574)
XLA Ops:
  8.0 35.4 %all-gather.3.cloned.1.call-done = bf16[20,48,1024]{2,1,0:T(8,128)(2,1)} async-done(((bf16[20,48,128]{2,1,0:T(8,128)(2,1)}), bf16[20,48,1024]{2,1,0:T(8,128)(2,1)}) %all-gather.3.cloned.1.call-update) | async-done | bytes 1966096 | tf_op jit(solution)/shard_map/all_gather | solution.py:17
  43.4 3.7 broadcast_select_fusion.1
  49.2 3.9 gather_fusion
  53.1 4.7 gather.7
  58.1 4.9 select_multiply_fusion
  63.0 144.0 %all-reduce.10.cloned.1.call-done = (bf16[20,48,1024]{2,1,0:T(8,128)(2,1)}, bf16[20,48,1024]{2,1,0:T(8,128)(2,1)}) async-done(((bf16[20,48,1024]{2,1,0:T(8,128)(2,1)}, bf16[20,48,1024]{2,1,0:T(8,128)(2,1)}), (bf16[20,48,1024]{2,1,0:T(8,128)(2,1)}, bf16[20,48,1024]{2,1,0:T(8,128)(2,1)})) %all-reduce.10.cloned.1.call-update) | async-done | bytes 3932176 | tf_op jit(solution)/shard_map/psum | solution.py:13
  207.0 4.6 pad_maximum_fusion
  211.6 157.5 %while.10 = (s32[]{:T(128)}, bf16[8,5,48,960]{3,2,1,0:T(8,128)(2,1)}, bf16[8,5,48,1024]{3,2,1,0:T(8,128)(2,1)}, f32[8,5,20,1024]{3,2,1,0:T(8,128)}, bf16[20,48,1024]{2,1,0:T(8,128)(2,1)S(1)}, /*index=5*/s32[]{:T(128)}) while((s32[]{:T(128)}, bf16[8,5,48,960]{3,2,1,0:T(8,128)(2,1)}, bf16[8,5,48,1024]{3,2,1,0:T(8,128)(2,1)}, ...), condition=%wide.region_3.4_spmd, body=%wide.region_2.3_spmd.sunk | while | flops 482903040 | bytes 31704136 | solution.py:49
  211.6 1.1 dynamic-slice_bitcast_fusion.2
  212.7 2.5 bitcast_convert_fusion.2
  215.2 8.6 %fusion.28 = bf16[5,960,1024]{2,1,0:T(8,128)(2,1)} fusion(f32[960,1024]{1,0:T(8,128)} %bitcast_convert_fusion.2, f32[5,20,1024]{2,1,0:T(8,128)S(1)} %dynamic-slice_bitcast_fusion.2), kind=kLoop, calls=%fused_computation.2.clone.1 | loop fusion | flops 9830400 | bytes 14172160 | tf_op jit(solution)/shard_map/while/body/eval_jaxpr/convert_element_type | solution.py:43
  223.7 7.6 %fusion.29 = bf16[8,5,48,960]{3,2,1,0:T(8,128)(2,1)} fusion(bf16[8,5,48,960]{3,2,1,0:T(8,128)(2,1)} %get-tuple-element.97, s32[]{:T(128)} %get-tuple-element.96, bf16[5,960,1024]{2,1,0:T(8,128)(2,1)} %fusion.28, bf16[8,5,48,1024]{3,2,1,0:T(8,128)(2,1)} %get-tuple-element.104), kind=kOutput, calls=%fused_computation.6.clone.1 | convolution fusion | flops 472089600 | bytes 10814464 | tf_op jit(solution)/shard_map/while/body/eval_jaxpr/akr,anr->akn/dot_general | solution.py:45
  231.3 1.1 dynamic-slice_bitcast_fusion.2
  232.4 2.5 bitcast_convert_fusion.2
  234.9 8.6 %fusion.28 = bf16[5,960,1024]{2,1,0:T(8,128)(2,1)} fusion(f32[960,1024]{1,0:T(8,128)} %bitcast_convert_fusion.2, f32[5,20,1024]{2,1,0:T(8,128)S(1)} %dynamic-slice_bitcast_fusion.2), kind=kLoop, calls=%fused_computation.2.clone.1 | loop fusion | flops 9830400 | bytes 14172160 | tf_op jit(solution)/shard_map/while/body/eval_jaxpr/convert_element_type | solution.py:43
  243.4 7.6 %fusion.29 = bf16[8,5,48,960]{3,2,1,0:T(8,128)(2,1)} fusion(bf16[8,5,48,960]{3,2,1,0:T(8,128)(2,1)} %get-tuple-element.97, s32[]{:T(128)} %get-tuple-element.96, bf16[5,960,1024]{2,1,0:T(8,128)(2,1)} %fusion.28, bf16[8,5,48,1024]{3,2,1,0:T(8,128)(2,1)} %get-tuple-element.104), kind=kOutput, calls=%fused_computation.6.clone.1 | convolution fusion | flops 472089600 | bytes 10814464 | tf_op jit(solution)/shard_map/while/body/eval_jaxpr/akr,anr->akn/dot_general | solution.py:45
  251.0 1.1 dynamic-slice_bitcast_fusion.2
  252.1 2.5 bitcast_convert_fusion.2
  254.5 8.6 %fusion.28 = bf16[5,960,1024]{2,1,0:T(8,128)(2,1)} fusion(f32[960,1024]{1,0:T(8,128)} %bitcast_convert_fusion.2, f32[5,20,1024]{2,1,0:T(8,128)S(1)} %dynamic-slice_bitcast_fusion.2), kind=kLoop, calls=%fused_computation.2.clone.1 | loop fusion | flops 9830400 | bytes 14172160 | tf_op jit(solution)/shard_map/while/body/eval_jaxpr/convert_element_type | solution.py:43
  263.1 7.6 %fusion.29 = bf16[8,5,48,960]{3,2,1,0:T(8,128)(2,1)} fusion(bf16[8,5,48,960]{3,2,1,0:T(8,128)(2,1)} %get-tuple-element.97, s32[]{:T(128)} %get-tuple-element.96, bf16[5,960,1024]{2,1,0:T(8,128)(2,1)} %fusion.28, bf16[8,5,48,1024]{3,2,1,0:T(8,128)(2,1)} %get-tuple-element.104), kind=kOutput, calls=%fused_computation.6.clone.1 | convolution fusion | flops 472089600 | bytes 10814464 | tf_op jit(solution)/shard_map/while/body/eval_jaxpr/akr,anr->akn/dot_general | solution.py:45
  270.7 1.1 dynamic-slice_bitcast_fusion.2
  271.7 2.5 bitcast_convert_fusion.2
  274.2 8.6 %fusion.28 = bf16[5,960,1024]{2,1,0:T(8,128)(2,1)} fusion(f32[960,1024]{1,0:T(8,128)} %bitcast_convert_fusion.2, f32[5,20,1024]{2,1,0:T(8,128)S(1)} %dynamic-slice_bitcast_fusion.2), kind=kLoop, calls=%fused_computation.2.clone.1 | loop fusion | flops 9830400 | bytes 14172160 | tf_op jit(solution)/shard_map/while/body/eval_jaxpr/convert_element_type | solution.py:43
  282.8 7.6 %fusion.29 = bf16[8,5,48,960]{3,2,1,0:T(8,128)(2,1)} fusion(bf16[8,5,48,960]{3,2,1,0:T(8,128)(2,1)} %get-tuple-element.97, s32[]{:T(128)} %get-tuple-element.96, bf16[5,960,1024]{2,1,0:T(8,128)(2,1)} %fusion.28, bf16[8,5,48,1024]{3,2,1,0:T(8,128)(2,1)} %get-tuple-element.104), kind=kOutput, calls=%fused_computation.6.clone.1 | convolution fusion | flops 472089600 | bytes 10814464 | tf_op jit(solution)/shard_map/while/body/eval_jaxpr/akr,anr->akn/dot_general | solution.py:45
  290.4 1.1 dynamic-slice_bitcast_fusion.2
  291.4 2.5 bitcast_convert_fusion.2
  293.9 8.6 %fusion.28 = bf16[5,960,1024]{2,1,0:T(8,128)(2,1)} fusion(f32[960,1024]{1,0:T(8,128)} %bitcast_convert_fusion.2, f32[5,20,1024]{2,1,0:T(8,128)S(1)} %dynamic-slice_bitcast_fusion.2), kind=kLoop, calls=%fused_computation.2.clone.1 | loop fusion | flops 9830400 | bytes 14172160 | tf_op jit(solution)/shard_map/while/body/eval_jaxpr/convert_element_type | solution.py:43
  302.5 7.6 %fusion.29 = bf16[8,5,48,960]{3,2,1,0:T(8,128)(2,1)} fusion(bf16[8,5,48,960]{3,2,1,0:T(8,128)(2,1)} %get-tuple-element.97, s32[]{:T(128)} %get-tuple-element.96, bf16[5,960,1024]{2,1,0:T(8,128)(2,1)} %fusion.28, bf16[8,5,48,1024]{3,2,1,0:T(8,128)(2,1)} %get-tuple-element.104), kind=kOutput, calls=%fused_computation.6.clone.1 | convolution fusion | flops 472089600 | bytes 10814464 | tf_op jit(solution)/shard_map/while/body/eval_jaxpr/akr,anr->akn/dot_general | solution.py:45
  310.1 1.1 dynamic-slice_bitcast_fusion.2
  311.2 2.5 bitcast_convert_fusion.2
  313.6 8.6 %fusion.28 = bf16[5,960,1024]{2,1,0:T(8,128)(2,1)} fusion(f32[960,1024]{1,0:T(8,128)} %bitcast_convert_fusion.2, f32[5,20,1024]{2,1,0:T(8,128)S(1)} %dynamic-slice_bitcast_fusion.2), kind=kLoop, calls=%fused_computation.2.clone.1 | loop fusion | flops 9830400 | bytes 14172160 | tf_op jit(solution)/shard_map/while/body/eval_jaxpr/convert_element_type | solution.py:43
  322.2 7.6 %fusion.29 = bf16[8,5,48,960]{3,2,1,0:T(8,128)(2,1)} fusion(bf16[8,5,48,960]{3,2,1,0:T(8,128)(2,1)} %get-tuple-element.97, s32[]{:T(128)} %get-tuple-element.96, bf16[5,960,1024]{2,1,0:T(8,128)(2,1)} %fusion.28, bf16[8,5,48,1024]{3,2,1,0:T(8,128)(2,1)} %get-tuple-element.104), kind=kOutput, calls=%fused_computation.6.clone.1 | convolution fusion | flops 472089600 | bytes 10814464 | tf_op jit(solution)/shard_map/while/body/eval_jaxpr/akr,anr->akn/dot_general | solution.py:45
  329.8 1.1 dynamic-slice_bitcast_fusion.2
  330.8 2.5 bitcast_convert_fusion.2
  333.3 8.6 %fusion.28 = bf16[5,960,1024]{2,1,0:T(8,128)(2,1)} fusion(f32[960,1024]{1,0:T(8,128)} %bitcast_convert_fusion.2, f32[5,20,1024]{2,1,0:T(8,128)S(1)} %dynamic-slice_bitcast_fusion.2), kind=kLoop, calls=%fused_computation.2.clone.1 | loop fusion | flops 9830400 | bytes 14172160 | tf_op jit(solution)/shard_map/while/body/eval_jaxpr/convert_element_type | solution.py:43
  341.9 7.6 %fusion.29 = bf16[8,5,48,960]{3,2,1,0:T(8,128)(2,1)} fusion(bf16[8,5,48,960]{3,2,1,0:T(8,128)(2,1)} %get-tuple-element.97, s32[]{:T(128)} %get-tuple-element.96, bf16[5,960,1024]{2,1,0:T(8,128)(2,1)} %fusion.28, bf16[8,5,48,1024]{3,2,1,0:T(8,128)(2,1)} %get-tuple-element.104), kind=kOutput, calls=%fused_computation.6.clone.1 | convolution fusion | flops 472089600 | bytes 10814464 | tf_op jit(solution)/shard_map/while/body/eval_jaxpr/akr,anr->akn/dot_general | solution.py:45
  349.5 1.1 dynamic-slice_bitcast_fusion.2
  350.5 2.5 bitcast_convert_fusion.2
  353.0 8.6 %fusion.28 = bf16[5,960,1024]{2,1,0:T(8,128)(2,1)} fusion(f32[960,1024]{1,0:T(8,128)} %bitcast_convert_fusion.2, f32[5,20,1024]{2,1,0:T(8,128)S(1)} %dynamic-slice_bitcast_fusion.2), kind=kLoop, calls=%fused_computation.2.clone.1 | loop fusion | flops 9830400 | bytes 14172160 | tf_op jit(solution)/shard_map/while/body/eval_jaxpr/convert_element_type | solution.py:43
  361.6 7.6 %fusion.29 = bf16[8,5,48,960]{3,2,1,0:T(8,128)(2,1)} fusion(bf16[8,5,48,960]{3,2,1,0:T(8,128)(2,1)} %get-tuple-element.97, s32[]{:T(128)} %get-tuple-element.96, bf16[5,960,1024]{2,1,0:T(8,128)(2,1)} %fusion.28, bf16[8,5,48,1024]{3,2,1,0:T(8,128)(2,1)} %get-tuple-element.104), kind=kOutput, calls=%fused_computation.6.clone.1 | convolution fusion | flops 472089600 | bytes 10814464 | tf_op jit(solution)/shard_map/while/body/eval_jaxpr/akr,anr->akn/dot_general | solution.py:45
  369.1 4.5 fusion.6
  373.7 144.7 %all-reduce.6.cloned.1.call-done = f32[1920,128]{1,0:T(8,128)} async-done(((f32[1920,128]{1,0:T(8,128)}), f32[1920,128]{1,0:T(8,128)}) %all-reduce.6.cloned.1.call-update) | async-done | bytes 983056 | tf_op jit(solution)/shard_map/psum | solution.py:60
  518.4 2.1 add_convert_fusion
  520.5 36.0 %all-gather.5.cloned.1.call-done = bf16[15360,128]{1,0:T(8,128)(2,1)} async-done(((bf16[1920,128]{1,0:T(8,128)(2,1)}), bf16[15360,128]{1,0:T(8,128)(2,1)}) %all-gather.5.cloned.1.call-update) | async-done | bytes 3932176 | tf_op jit(solution)/shard_map/all_gather | solution.py:64
  556.6 4.4 fusion.7
  563.0 6.2 copy.20
  569.2 136.3 %all-reduce.8.cloned.1.call-done = f32[1920,128]{0,1:T(8,128)} async-done(((f32[1920,128]{0,1:T(8,128)}), f32[1920,128]{0,1:T(8,128)}) %all-reduce.8.cloned.1.call-update) | async-done | bytes 983056
  705.5 1.4 dynamic-slice_add_fusion
  (42 shorter events, 4.5 us)
Async XLA Ops:
  7.2 42.0 %copy-start = (f32[256,1024]{1,0:T(8,128)S(1)}, f32[256,1024]{1,0:T(8,128)}, u32[]{:S(2)}) copy-start(f32[256,1024]{1,0:T(8,128)} %param.10) | copy-start | bytes 3145732
  7.2 36.2 %all-gather.3.cloned.1.call-start = ((), (), s32[]{:S(2)}) async-start(), calls=%async_computation | async-start | bytes 2211840 | tf_op jit(solution)/shard_map/all_gather | solution.py:17
  7.9 199.1 %all-reduce.10.cloned.1.call-start = ((), (), s32[]{:S(2)}) async-start(), calls=%async_computation.4 | async-start | bytes 7864320 | tf_op jit(solution)/shard_map/psum | solution.py:13
  8.0 40.9 %copy-start.4 = (s32[40,20]{0,1:T(8,128)S(1)}, s32[40,20]{0,1:T(8,128)}, u32[]{:S(2)}) copy-start(s32[40,20]{0,1:T(8,128)} %param.11) | copy-start | bytes 9604
  47.1 471.2 %all-reduce.6.cloned.1.call-start = ((), (), s32[]{:S(2)}) async-start(), calls=%async_computation.1 | async-start | bytes 1966080 | tf_op jit(solution)/shard_map/psum | solution.py:60
  53.1 4.8 copy-start.5
  207.0 4.6 copy-start.1
  369.1 149.2 %copy-start.2 = (f32[1920,128]{1,0:T(8,128)S(1)}, f32[1920,128]{1,0:T(8,128)}, u32[]{:S(2)}) copy-start(f32[1920,128]{1,0:T(8,128)} %param.15) | copy-start | bytes 2949124
  369.1 187.5 %copy-start.3 = (bf16[960,128]{1,0:T(8,128)(2,1)S(1)}, bf16[960,128]{1,0:T(8,128)(2,1)}, u32[]{:S(2)}) copy-start(bf16[960,128]{1,0:T(8,128)(2,1)} %param.14) | copy-start | bytes 737284
  373.6 183.0 %all-gather.5.cloned.1.call-start = ((), (), s32[]{:S(2)}) async-start(), calls=%async_computation.2 | async-start | bytes 4423680 | tf_op jit(solution)/shard_map/all_gather | solution.py:64
  520.5 185.0 %all-reduce.8.cloned.1.call-start = ((), (), s32[]{:S(2)}) async-start(), calls=%async_computation.3 | async-start | bytes 1966080
  561.0 0.7 copy-start.6
Sparse Core Ops, SparseCore 0:
  9.8 33.4 all-gather.2
  47.3 159.6 all-reduce.9
  373.7 144.5 all-reduce.5
  520.6 35.8 all-gather.4
  561.2 144.2 all-reduce.7
where the time goes:
time: 718 us; the launch traced here: 713 us
  waiting for transfers between devices  497 us (69%)
  other arithmetic  105 us (15%)
  matrix products  69.7 us (10%)
  local copies, waits for them, and re-layouts  26.6 us (4%)
  between operations  14.6 us (2%)
    psum x1, waiting for transfers between devices, body(): summed = lax.psum(partial_value, 'col')  145 us
    psum x1, waiting for transfers between devices, broadcast(): return lax.psum(kept, axis)  144 us
    unnamed x6, waiting for transfers between devices  137 us
    convert_element_type x8, other arithmetic, build_rows(): (weight_rows[:, :, None, :] * col_panel[None, :, :, :]).astype(jnp.bfloat16)  68.4 us
    dot_general x8, matrix products, build_rows(): jnp.einsum('akr,anr->akn', panel_rows, scaled, preferred_element_type=jnp...  60.8 us
    all_gather x1, waiting for transfers between devices, body(): gathered = lax.all_gather(first_iterate, 'row', axis=0, tiled=True)  36 us
    all_gather x1, waiting for transfers between devices, body(): col_panel = lax.all_gather(radial, 'row', axis=2, tiled=True)  35.4 us
    convert_element_type x8, other arithmetic, build_rows(): weight_rows[:, :, None, :] * col_panel[None, :, :, :]  19.8 us
  transfers between devices with their start and end apart: 5, of which 5 were waited for; matrix products, arithmetic and copies ran while one was open for 3% of the time, Pallas kernels for 0%

commit v1 on v0

v1 whole, which is shorter than its diff:
```python
import functools

import jax
import jax.numpy as jnp
from jax import lax
from jax.experimental import pallas as pl
from jax.experimental.pallas import tpu as pltpu
from jax.sharding import PartitionSpec as P

NTARG = 4
MESH = pl.DeviceIdType.MESH
BF, F32 = jnp.bfloat16, jnp.float32

NX, NZ, NY = 4, 8, 4
NROW = 8
MOM = 48
GRID = 1024
LANE = 128
NB = 20
GRP = 10
HALF = 5
HROW = HALF * MOM
GROW = GRP * MOM
COLS = NB * MOM
ROWS = 4 * GROW
SH = 64
WIN = 4
NWIN = NB // WIN


def kernel(idx_ref, ang_ref, rad_ref, form_ref, gb_ref, kmat_ref, born_ref,
           v_out, first_out, share_out,
           table, colp, rowp, vbuf, weighted, pown, psend, precv, ssum, zsend, zrecv, bornp,
           fi, upd, t32, t16, pbuf, txrecv, tz32, tzsend, tzrecv,
           sc_s, sc_r, y_s, y_r, z_s, z_r, x_s, x_r, p_s, p_r, r_s, r_r, u_s, u_r,
           fz_s, fz_r, fx_s, fx_r, tx_s, tx_r, tz_s, tz_r, out_s):
    row = lax.axis_index("row")
    col = lax.axis_index("col")
    x, z = col // NZ, col % NZ
    y, core = row // 2, row % 2

    def at_x(d):
        return (row, lax.rem(x + d, NX) * NZ + z)

    def at_z(d):
        return (row, x * NZ + lax.rem(z + d, NZ))

    def at_y(d):
        return (lax.rem(y + d, NY) * 2 + core, col)

    sibling = (y * 2 + 1 - core, col)
    in_slab = col < 2 * NROW
    panel_row, part = col // 2, col % 2

    def scatter_to(h):
        return (panel_row, (2 * part + h) * NZ + row)

    def scatter_self(h):
        return (panel_row == row) & ((2 * part + h) * NZ + row == col)

    use_col = 2 * row + x // 2
    use_self = use_col == col
    source_self = (col // 2 == row) & (x // 2 == part)

    def copy(src, dst, ss, rs, dev):
        return pltpu.make_async_remote_copy(src_ref=src, dst_ref=dst, send_sem=ss, recv_sem=rs,
                                            device_id=dev, device_id_type=MESH)

    bar = pltpu.get_barrier_semaphore()

    def greet(dev):
        pl.semaphore_signal(bar, inc=1, device_id=dev, device_id_type=MESH)

    for d in range(1, NZ):
        greet(at_z(d))
    for d in range(1, NX):
        greet(at_x(d))
    greet(at_y(1))
    greet(at_y(3))
    greet(sibling)
    sc_src_row, sc_src_col = z, 2 * row + x // 2
    sc_from_self = (sc_src_row == row) & (sc_src_col == col)

    @pl.when(jnp.logical_not(sc_from_self))
    def _():
        greet((sc_src_row, sc_src_col))

    @pl.when(in_slab)
    def _():
        def hello(k, carry):
            g, zz = 2 * part + k // NZ, lax.rem(k, NZ)
            me = (panel_row == row) & (g * NZ + zz == col)

            @pl.when(jnp.logical_not(me))
            def _():
                greet((panel_row, g * NZ + zz))
            return carry

        lax.fori_loop(0, 2 * NZ, hello, 0)

    colp[:, COLS:, :] = jnp.zeros((NROW, 1024 - COLS, LANE), BF)
    zsend[GROW:, :] = jnp.zeros((NZ * SH - GROW, LANE), BF)
    ssum[GROW:, :] = jnp.zeros((NZ * SH - GROW, LANE), F32)
    bornp[GROW:, :] = jnp.zeros((NZ * SH - GROW, LANE), F32)
    t32[:, 60:, :] = jnp.zeros((NX * NZ, 4, LANE), F32)

    n_wait = 7 + 3 + 3 + 8 - use_self.astype(jnp.int32)
    n_wait = n_wait + jnp.where(in_slab, 2 - scatter_self(0).astype(jnp.int32) - scatter_self(1).astype(jnp.int32), 0)
    pl.semaphore_wait(bar, n_wait)

    def sc_copy(h, half):
        p = 2 * h + half
        return copy(rad_ref.at[pl.ds(p * HROW, HROW)], rowp.at[2 * part + h, half, row], sc_s.at[p], sc_r.at[half],
                    scatter_to(h))

    for half in range(2):
        for h in range(2):
            @pl.when(in_slab & jnp.logical_not(scatter_self(h)))
            def _():
                sc_copy(h, half).start()

            @pl.when(in_slab & scatter_self(h))
            def _():
                rowp[2 * part + h, half, row] = rad_ref[(2 * h + half) * HROW:(2 * h + half + 1) * HROW, :]

    below, above = lax.rem(y + 3, NY) * 2 + core, lax.rem(y + 1, NY) * 2 + core
    across = lax.rem(y + 2, NY) * 2 + core
    lo, hi = pl.ds(0, GROW), pl.ds(GROW, GROW)
    whole = pl.ds(0, COLS)

    def y_copy(k, src, dst, dev):
        return copy(src, dst, y_s.at[k], y_r.at[k], dev)

    def slot(r, part_):
        return colp.at[r, part_]

    ys = [
        y_copy(0, rad_ref, slot(row, whole), at_y(1)),
        y_copy(1, rad_ref, slot(row, whole), at_y(3)),
        y_copy(2, rad_ref, slot(row, whole), sibling),
        y_copy(3, slot(below, lo), slot(below, lo), at_y(1)),
        y_copy(4, slot(above, hi), slot(above, hi), at_y(3)),
        y_copy(5, slot(below, whole), slot(below, whole), sibling),
        y_copy(6, slot(above, whole), slot(above, whole), sibling),
        y_copy(7, slot(across, lo), slot(across, lo), sibling),
        y_copy(8, slot(across, hi), slot(across, hi), sibling),
    ]
    ys[0].start()
    ys[1].start()
    ys[2].start()
    colp[row, 0:COLS, :] = rad_ref[...]

    def flow_at(f):
        if f == 0:
            return x, 0
        return lax.rem(x + f - 1, NX), 1

    def steps(f, sign):
        return 4 if (f <= 2) == (sign > 0) else 3

    def z_copy(f, sign, s):
        g, half = flow_at(f)
        origin = lax.rem(z + (NZ - s if sign > 0 else s), NZ)
        k = (f * 2 + (0 if sign > 0 else 1)) * 4 + s
        ref = rowp.at[g, half, origin]
        return copy(ref, ref, z_s.at[k], z_r.at[k], at_z(1 if sign > 0 else NZ - 1))

    def z_wait(f, sign, s):
        z_copy(f, sign, s).wait_recv()
        if s + 1 < steps(f, sign):
            z_copy(f, sign, s + 1).start()

    def piece(k):
        d = (k + 1) // 2
        return lax.rem(z + (NZ - d if k % 2 == 1 else d), NZ)

    def xh2(k, sign):
        ref = rowp.at[x, 0, piece(k)]
        n = k if sign > 0 else 8 + k
        return copy(ref, ref, x_s.at[n], x_r.at[n], at_x(1 if sign > 0 else 3))

    def xh2_forward(k):
        sign = 1 if k % 2 == 0 else -1
        ref = rowp.at[lax.rem(x + (3 if sign > 0 else 1), NX), 0, piece(k)]
        return copy(ref, ref, x_s.at[16 + k], x_r.at[16 + k], at_x(1 if sign > 0 else 3))

    def xh2_start(k):
        xh2(k, 1).start()
        xh2(k, -1).start()

    def xh2_wait(k):
        xh2(k, 1).wait_recv()
        xh2(k, -1).wait_recv()
        xh2_forward(k).start()

    def xh1(n):
        ref = rowp.at[lax.rem(x + (3 if n == 2 else 0), NX), 1, z]
        return copy(ref, ref, x_s.at[24 + n], x_r.at[24 + n], at_x(3 if n == 1 else 1))

    def flow_start(f):
        z_copy(f, 1, 0).start()
        z_copy(f, -1, 0).start()

    def sc_wait(half):
        @pl.when(jnp.logical_not(sc_from_self))
        def _():
            sc_copy(0, half).wait_recv()

    sc_wait(0)
    flow_start(0)
    xh2_start(0)
    sc_wait(1)
    flow_start(1)
    xh1(0).start()
    xh1(1).start()

    def spread(i, carry):
        table[i] = jnp.broadcast_to(form_ref[pl.ds(i, 1), :], (16, GRID)).astype(BF)
        return carry

    lax.fori_loop(0, 128, spread, 0, unroll=4)
    ys[0].wait_recv()
    ys[1].wait_recv()
    ys[3].start()
    ys[4].start()
    ys[5].start()
    ys[6].start()
    z_wait(0, 1, 0)
    xh2_start(1)
    z_wait(0, -1, 0)
    xh2_start(2)
    xh1(0).wait_recv()
    xh1(2).start()
    flow_start(4)
    xh1(1).wait_recv()
    flow_start(2)
    xh2_wait(0)
    z_wait(1, 1, 0)
    z_wait(1, -1, 0)
    lax.fori_loop(128, 256, spread, 0, unroll=4)
    z_wait(0, 1, 1)
    xh2_start(3)
    z_wait(0, -1, 1)
    xh2_start(4)
    xh1(2).wait_recv()
    flow_start(3)
    xh2_wait(1)
    xh2_wait(2)
    weighted[...] = (gb_ref[...] * kmat_ref[...].astype(F32)).astype(BF)
    bornp[0:GROW, :] = born_ref[pl.ds(x * GROW, GROW), :]
    z_wait(0, 1, 2)
    xh2_start(5)
    z_wait(0, -1, 2)
    xh2_start(6)
    z_wait(1, 1, 1)
    z_wait(1, -1, 1)
    z_wait(0, 1, 3)
    xh2_start(7)
    ys[3].wait_recv()
    ys[4].wait_recv()
    ys[7].start()
    ys[8].start()
    for f in (4, 2):
        z_wait(f, 1, 0)
        z_wait(f, -1, 0)
    for k in (2, 5, 6, 7, 8):
        ys[k].wait_recv()

    def before_1():
        z_wait(1, 1, 2)
        z_wait(1, -1, 2)
        xh2_wait(3)
        xh2_wait(4)
        z_wait(3, 1, 0)
        z_wait(3, -1, 0)
        z_wait(1, 1, 3)

    def before_2():
        for f in (4, 2):
            z_wait(f, 1, 1)
            z_wait(f, -1, 1)
        for k in (5, 6, 7):
            xh2_wait(k)

    def before_3():
        z_wait(3, 1, 1)
        z_wait(3, -1, 1)

    def before_4():
        for f in (4, 2):
            z_wait(f, 1, 2)
            z_wait(f, -1, 2)
        for k in range(8):
            xh2_forward(k).wait_recv()

    def before_5():
        z_wait(3, 1, 2)
        z_wait(3, -1, 2)
        z_wait(2, 1, 3)

    def before_6():
        z_wait(4, -1, 3)

    def before_7():
        z_wait(3, -1, 3)

    befores = {1: before_1, 2: before_2, 3: before_3, 4: before_4, 5: before_5, 6: before_6, 7: before_7}

    def p_copy(d, half):
        n = (d - 1) * 2 + half
        return copy(psend.at[n], precv.at[n], p_s.at[n], p_r.at[n], at_x(d))

    def v_copy(t, g, half):
        rows = pl.ds(pl.multiple_of(g * GROW + half * HROW, HROW), HROW)
        return pltpu.make_async_copy(vbuf.at[rows], v_out.at[rows], out_s.at[t])

    def batch(t):
        late = jnp.maximum(t - 2, 0)
        third = lax.rem(late, 3)
        d = jnp.where(t < 2, 0, jnp.where(third == 0, 1, jnp.where(third == 1, 3, 2)))
        half = jnp.where((t == 1) | (t >= 5), 1, 0)
        return d, lax.rem(x + d, NX), half

    lanes = lax.broadcasted_iota(jnp.int32, (MOM, 256), 1)

    def build(t, carry):
        for k, fn in befores.items():
            pl.when(t == k)(fn)
        d, g, half = batch(t)
        first = g * GRP + half * HALF
        for w in range(NWIN):
            base = w * WIN * MOM
            start = base // LANE * LANE
            off = base - start
            width = min(256, COLS - start)
            win = jnp.concatenate([colp[c, start:start + 256, :] for c in range(8)], axis=1)
            parts = []
            for i in range(HALF):
                chan = jnp.concatenate(
                    [rowp[g, half, c, i * MOM:(i + 1) * MOM, :] for c in range(8)], axis=1
                ).reshape(3, 16, GRID)
                for j in range(WIN):
                    factor = table[idx_ref[first + i, w * WIN + j]]
                    parts.append((chan * factor[None]).reshape(MOM, GRID))
            scaled = jnp.concatenate(parts, axis=0)
            prod = lax.dot_general(scaled, win, (((1,), (1,)), ((), ())), preferred_element_type=F32)
            for i in range(HALF):
                acc = jnp.zeros((MOM, 256), F32)
                for j in range(WIN):
                    n = i * WIN + j
                    low = off + j * MOM
                    mine = prod[n * MOM:(n + 1) * MOM] * ang_ref[first + i, w * WIN + j]
                    acc = jnp.where((lanes >= low) & (lanes < low + MOM), mine, acc)
                rows = pl.ds(pl.multiple_of((first + i) * MOM, MOM), MOM)
                new = acc.astype(BF)
                if off:
                    new = jnp.where(lanes >= off, new, vbuf[rows, start:start + width])
                vbuf[rows, start:start + width] = new[:, :width]
        rows = pl.ds(pl.multiple_of(g * GROW + half * HROW, HROW), HROW)
        v_copy(t, g, half).start()
        part_sum = jnp.dot(vbuf[rows, :], weighted[...], preferred_element_type=F32)

        @pl.when(d == 0)
        def _():
            pown[half] = part_sum

        @pl.when(d > 0)
        def _():
            n = (d - 1) * 2 + half
            psend[n] = part_sum.astype(BF)
            p_copy(d, half).start()
        return carry

    lax.fori_loop(0, 8, build, 0)

    def tx_copy(d):
        to = lax.rem(x + d, NX)
        return copy(t16.at[pl.ds(to * NZ, NZ)], txrecv.at[d - 1], tx_s.at[d], tx_r.at[d], at_x(d))

    def second(operand):
        turned = operand.T.astype(BF)

        def chunk(q, carry):
            rows = pl.ds(pl.multiple_of(q * 384, 384), 384)
            prod = lax.dot_general(turned, vbuf[rows, :], (((1,), (1,)), ((), ())), preferred_element_type=F32)
            for jj in range(3):
                pbuf[jj] = prod[:, jj * LANE:(jj + 1) * LANE]
            for jj in range(3):
                for c in range(NX * NZ):
                    t32[c, pl.ds(q * 12 + jj * 4, 4), :] = pbuf[jj, 4 * c:4 * c + 4, :]
            return carry

        lax.fori_loop(0, 5, chunk, 0)
        t16[...] = t32[...].astype(BF)
        for d in (2, 1, 3):
            tx_copy(d).start()

    @pl.when(jnp.logical_not(in_slab))
    def _():
        second(weighted[...].astype(F32))

    for n in range(6):
        p_copy(n // 2 + 1, n % 2).wait_recv()
    for half in range(2):
        total = pown[half]
        for d in range(3):
            total = total + precv[d * 2 + half].astype(F32)
        ssum[half * HROW:(half + 1) * HROW, :] = total
        zsend[half * HROW:(half + 1) * HROW, :] = total.astype(BF)

    def shard(q):
        return pl.ds(pl.multiple_of(q * SH, SH), SH)

    def r_copy(d):
        return copy(zsend.at[shard(lax.rem(z + d, NZ))], zrecv.at[d - 1], r_s.at[d], r_r.at[d], at_z(d))

    for d in range(1, NZ):
        r_copy(d).start()
    for d in range(1, NZ):
        r_copy(d).wait_recv()
    total = bornp[shard(z), :] + ssum[shard(z), :]
    for d in range(NZ - 1):
        total = total + zrecv[d].astype(F32)
    fresh = total.astype(BF)
    fi[x, shard(z), :] = fresh
    g_part = lax.rem(x, 2)

    def u_copy(k):
        src = fi.at[x, shard(z)]
        return copy(src, upd.at[g_part, shard(z)], u_s.at[k], u_r.at[g_part * NZ + z], (lax.rem(row + k, NROW), use_col))

    for k in range(NROW):
        if k == 0:
            @pl.when(use_self)
            def _():
                upd[g_part, shard(z), :] = fresh

            @pl.when(jnp.logical_not(use_self))
            def _():
                u_copy(0).start()
        else:
            u_copy(k).start()

    def fz_copy(d):
        ref = fi.at[x, shard(z)]
        return copy(ref, ref, fz_s.at[d], fz_r.at[d], at_z(d))

    for d in range(1, NZ):
        fz_copy(d).start()

    @pl.when(in_slab)
    def _():
        for k in range(2 * NZ):
            ref = upd.at[k // NZ, pl.ds(k % NZ * SH, SH)]

            @pl.when(jnp.logical_not(source_self & (g_part * NZ + z == k)))
            def _():
                copy(ref, ref, u_s.at[0], u_r.at[k], sibling).wait_recv()
        fresh_rows = jnp.concatenate([upd[0, 0:GROW, :], upd[1, 0:GROW, :]], axis=0)
        second((gb_ref[...] * fresh_rows.astype(F32)).astype(BF).astype(F32))

    for d in range(1, NZ):
        ref = fi.at[x, shard(lax.rem(z + NZ - d, NZ))]
        copy(ref, ref, fz_s.at[d], fz_r.at[d], at_z(d)).wait_recv()

    def fx_copy(d, g):
        ref = fi.at[g, pl.ds(0, GROW)]
        return copy(ref, ref, fx_s.at[d], fx_r.at[d], at_x(d))

    for d in (2, 1, 3):
        fx_copy(d, x).start()

    for d in range(1, NX):
        tx_copy(d).wait_recv()
    total = t32[pl.ds(x * NZ, NZ)]
    for d in range(NX - 1):
        total = total + txrecv[d].astype(F32)
    tz32[...] = total
    tzsend[...] = total.astype(BF)

    def tz_copy(d):
        return copy(tzsend.at[lax.rem(z + d, NZ)], tzrecv.at[d - 1], tz_s.at[d], tz_r.at[d], at_z(d))

    for d in range(1, NZ):
        tz_copy(d).start()
    for d in range(1, NX):
        fx_copy(d, lax.rem(x + NX - d, NX)).wait_recv()

    def f_out(g):
        return pltpu.make_async_copy(fi.at[g, pl.ds(0, GROW)], first_out.at[pl.ds(g * GROW, GROW)], out_s.at[8 + g])

    for g in range(NX):
        f_out(g).start()
    for d in range(1, NZ):
        tz_copy(d).wait_recv()
    total = tz32[z]
    for d in range(NZ - 1):
        total = total + tzrecv[d].astype(F32)
    share_out[...] = total

    for g in range(NX):
        f_out(g).wait()

    def v_wait(t, carry):
        _, g, half = batch(t)
        v_copy(t, g, half).wait()
        return carry

    lax.fori_loop(0, 8, v_wait, 0)
    for h in range(2):
        @pl.when(in_slab & jnp.logical_not(scatter_self(h)))
        def _():
            for half in range(2):
                sc_copy(h, half).wait_send()
    for c in ys:
        c.wait_send()
    for f in range(5):
        for sign in (1, -1):
            for s in range(steps(f, sign)):
                z_copy(f, sign, s).wait_send()
    for k in range(8):
        xh2(k, 1).wait_send()
        xh2(k, -1).wait_send()
        xh2_forward(k).wait_send()
    for n in range(3):
        xh1(n).wait_send()
    for n in range(6):
        p_copy(n // 2 + 1, n % 2).wait_send()
    for d in range(1, NZ):
        r_copy(d).wait_send()
        fz_copy(d).wait_send()
        tz_copy(d).wait_send()
    for d in range(1, NX):
        fx_copy(d, x).wait_send()
        tx_copy(d).wait_send()

    @pl.when(jnp.logical_not(use_self))
    def _():
        u_copy(0).wait_send()

    for k in range(1, NROW):
        u_copy(k).wait_send()


def body(radial, form_factors, coupling, quantum, green_diag, kmatrix, born_term):
    row_count, col_count = coupling.shape
    row_index, col_index = lax.axis_index("row"), lax.axis_index("col")
    rq = lax.dynamic_slice_in_dim(quantum, row_index * row_count, row_count, 0)
    cq = lax.dynamic_slice_in_dim(quantum, col_index * col_count, col_count, 0)
    table_index = coupling * (NTARG * NTARG) + rq[:, 2:3] * NTARG + cq[:, 2][None, :]
    parity = (rq[:, 0:1] + cq[:, 0][None, :]) % 2
    spread_m = jnp.abs(rq[:, 1:2] - cq[:, 1][None, :])
    angular = (1.0 - 2.0 * parity.astype(F32)) / (1.0 + spread_m.astype(F32))
    green = jnp.broadcast_to(green_diag.reshape(COLS, 1), (COLS, LANE))
    vm = pl.BlockSpec(memory_space=pltpu.VMEM)
    sm = pl.BlockSpec(memory_space=pltpu.SMEM)
    hb = pl.BlockSpec(memory_space=pl.ANY)
    dma = pltpu.SemaphoreType.DMA
    v_block, first, share = pl.pallas_call(
        kernel,
        out_shape=(
            jax.ShapeDtypeStruct((ROWS, COLS), BF),
            jax.ShapeDtypeStruct((ROWS, LANE), BF),
            jax.ShapeDtypeStruct((SH, LANE), F32),
        ),
        in_specs=[sm, sm, vm, vm, vm, vm, vm],
        out_specs=(hb, hb, vm),
        scratch_shapes=[
            pltpu.VMEM((256, 16, GRID), BF),
            pltpu.VMEM((NROW, 1024, LANE), BF),
            pltpu.VMEM((NX, 2, NROW, HROW, LANE), BF),
            pltpu.VMEM((ROWS, COLS), BF),
            pltpu.VMEM((COLS, LANE), BF),
            pltpu.VMEM((2, HROW, LANE), F32),
            pltpu.VMEM((6, HROW, LANE), BF),
            pltpu.VMEM((6, HROW, LANE), BF),
            pltpu.VMEM((NZ * SH, LANE), F32),
            pltpu.VMEM((NZ * SH, LANE), BF),
            pltpu.VMEM((NZ - 1, SH, LANE), BF),
            pltpu.VMEM((NZ * SH, LANE), F32),
            pltpu.VMEM((NX, NZ * SH, LANE), BF),
            pltpu.VMEM((2, NZ * SH, LANE), BF),
            pltpu.VMEM((NX * NZ, SH, LANE), F32),
            pltpu.VMEM((NX * NZ, SH, LANE), BF),
            pltpu.VMEM((3, LANE, LANE), F32),
            pltpu.VMEM((NX - 1, NZ, SH, LANE), BF),
            pltpu.VMEM((NZ, SH, LANE), F32),
            pltpu.VMEM((NZ, SH, LANE), BF),
            pltpu.VMEM((NZ - 1, SH, LANE), BF),
            dma((4,)), dma((2,)), dma((9,)), dma((9,)), dma((40,)), dma((40,)), dma((27,)), dma((27,)),
            dma((6,)), dma((6,)), dma((8,)), dma((8,)), dma((8,)), dma((16,)),
            dma((8,)), dma((8,)), dma((4,)), dma((4,)), dma((4,)), dma((4,)), dma((8,)), dma((8,)), dma((12,)),
        ],
        compiler_params=pltpu.CompilerParams(collective_id=0, has_side_effects=True, vmem_limit_bytes=56 << 20),
        name="sweeps",
    )(table_index, angular, radial.reshape(COLS, LANE), form_factors, green, kmatrix, born_term)
    born_share = lax.dynamic_slice_in_dim(born_term, col_index * 4, 4, 1)
    col_share = share[:60].reshape(15, 4, LANE).transpose(0, 2, 1).reshape(ROWS, 4)
    return v_block, first, born_share + col_share


def solution(mesh):
    placed = (
        P("col", None, "row"),
        P(),
        P("row", "col"),
        P(),
        P("col", None),
        P("col", None),
        P("row", None),
    )
    return jax.shard_map(
        body,
        mesh=mesh,
        in_specs=placed,
        out_specs=(P("row", "col"), P("row", None), P("row", "col")),
        check_vma=False,
    )
```

time: 718 us -> 147 us (0.20)
  waiting for transfers between devices: 497 us -> 0 us
  Pallas kernels: 0 us -> 131 us
  other arithmetic: 105 us -> 2.04 us
  matrix products: 69.7 us -> 0 us
  local copies, waits for them, and re-layouts: 26.6 us -> 11.2 us
  between operations: 14.6 us -> 0.7 us
    psum x2 -> x0, waiting for transfers between devices: 289 us -> none  [the longest x1 145 us: body(): summed = lax.psum(partial_value, 'col')]
    unnamed x6 -> x0, waiting for transfers between devices: 137 us -> none
    pallas_call x0 -> x1, Pallas kernels: none -> 131 us  [body(): pl.pallas_call(kernel, out_shape=(jax.ShapeDtypeStruct((ROWS, COLS), BF),...]
    convert_element_type x17 -> x0, other arithmetic: 90.3 us -> none  [the longest x8 68.4 us: build_rows(): (weight_rows[:, :, None, :] * col_panel[None, :, :, :]).astype(jnp.bfloat16)]
    all_gather x2 -> x0, waiting for transfers between devices: 71.4 us -> none  [the longest x1 36 us: body(): gathered = lax.all_gather(first_iterate, 'row', axis=0, tiled=True)]
    dot_general x10 -> x0, matrix products: 69.7 us -> none  [the longest x8 60.8 us: build_rows(): jnp.einsum('akr,anr->akn', panel_rows, scaled, preferred_element_type=jnp...]
    mul x9 -> x0, local copies, waits for them, and re-layouts: 8.57 us -> none  [the longest x8 8.49 us: build_rows(): weight_rows[:, :, None, :] * col_panel[None, :, :, :]]
    gather x2 -> x0, local copies, waits for them, and re-layouts: 8.53 us -> none  [body(): weights = jnp.take(form_factors, table_index, axis=0) * angular[:, :, None]]
  transfers between devices with their start and end apart: 5 -> 0, of which waited for: 5 -> 0; matrix products, arithmetic and copies ran while one was open for 3% -> 0% of each run, Pallas kernels for 0% -> 0%
where the time goes in v1:
time: 147 us; the launch traced here: 145 us
  Pallas kernels  131 us (89%)
  local copies, waits for them, and re-layouts  11.2 us (8%)
  other arithmetic  2.04 us (1%)
    pallas_call x1, Pallas kernels, body(): pl.pallas_call(kernel, out_shape=(jax.ShapeDtypeStruct((ROWS, COLS), BF),...  131 us
    unnamed x12, local copies, waits for them, and re-layouts  8.91 us

profile of v1, /device:TPU:1, one launch (start us, length us, event | category | flops | bytes accessed | tf_op | source)
XLA Modules:
  0.0 145.2 jit_solution(16853640855564836633)
XLA Ops:
  0.6 0.0 copy-start
  0.7 0.7 copy-done
  1.3 0.1 constant_dynamic-slice_fusion.1
  1.4 0.1 constant_dynamic-slice_fusion.2
  1.5 0.7 fusion.3.ang_ref
  2.2 0.8 copy.18
  3.0 0.7 add_add_fusion.idx_ref
  3.7 0.8 broadcast_in_dim.7
  4.4 1.0 broadcast_in_dim.8.gb_ref
  5.4 131.3 %sweeps.1 = (bf16[1920,960]{1,0:T(8,128)(2,1)}, bf16[1920,128]{1,0:T(8,128)(2,1)}, f32[64,128]{1,0:T(8,128)}) custom-call(s32[40,20]{1,0:T(8,128)} %add_add_fusion.idx_ref, f32[40,20]{1,0:T(8,128)} %fusion.3.ang_ref, bf16[960,128]{1,0:T(8,128)(2,1)} %bitcast.22, f32[256,1024]{1,0:T(8,128)} %form_ref.1, f32[960,128]{1,0:T(8,128)} %broadcast_in_dim.8.gb_ref, ...), custom_call_target="tpu_custom_call" | custom-call | tf_op jit(solution)/shard_map/sweeps/pallas_call | solution.py:559
  136.7 0.0 copy-start.3
  136.7 0.0 copy-start.1
  136.7 0.0 copy-start.2
  136.8 6.3 %copy.22 = bf16[1920,960]{0,1:T(8,128)(2,1)} copy(bf16[1920,960]{1,0:T(8,128)(2,1)} %get-tuple-element.15) | data formatting | bytes 7372800
  143.1 0.0 copy-done.3
  143.1 0.0 copy-done.1
  143.1 0.3 constant_dynamic-slice_fusion
  143.4 0.3 copy.23
  143.8 0.7 bitcast_add_fusion
  144.4 0.0 copy-done.2
  144.4 0.8 copy.29
  (4 shorter events, 0.0 us)
Async XLA Ops:
  0.6 0.7 copy-start
  136.7 6.4 %copy-start.3 = (f32[64,128]{1,0:T(8,128)S(1)}, f32[64,128]{1,0:T(8,128)}, u32[]{:S(2)}) copy-start(f32[64,128]{1,0:T(8,128)} %get-tuple-element.8) | copy-start | bytes 98308
  136.7 6.4 %copy-start.1 = (f32[1920,128]{1,0:T(8,128)S(1)}, f32[1920,128]{1,0:T(8,128)}, u32[]{:S(2)}) copy-start(f32[1920,128]{1,0:T(8,128)} %born_ref.1) | copy-start | bytes 2949124
  136.7 7.7 %copy-start.2 = (bf16[1920,128]{1,0:T(8,128)(2,1)S(1)}, bf16[1920,128]{1,0:T(8,128)(2,1)}, u32[]{:S(2)}) copy-start(bf16[1920,128]{1,0:T(8,128)(2,1)} %get-tuple-element.28) | copy-start | bytes 1474564

commit v2 on v1

v2 whole, which is shorter than its diff:
```python
import functools

import jax
import jax.numpy as jnp
from jax import lax
from jax.experimental import pallas as pl
from jax.experimental.pallas import tpu as pltpu
from jax.sharding import PartitionSpec as P

NTARG = 4
MESH = pl.DeviceIdType.MESH
BF, F32 = jnp.bfloat16, jnp.float32

NX, NZ, NY = 4, 8, 4
NROW = 8
MOM = 48
GRID = 1024
LANE = 128
NB = 20
HALF = 5
HROW = HALF * MOM
COLS = NB * MOM
MID = COLS // 2
ROWS = 2 * COLS
SH = 64
PAD = 4 * SH
WIN = 4
NWIN = NB // WIN


def kernel(code_ref, rad_ref, form_hbm, green_ref, kmat_ref, born_hbm,
           v_out, first_out, share_out,
           sign, table, form_ref, colp, rowp, mid, vbuf, vturn, gb_ref, weighted, pown, psend, precv, ssum, zsend, zrecv,
           born_ref, bornp, bturn, fi, upd, t32, t16, pbuf, txrecv, tz32, tzsend, tzrecv,
           s1_s, s1_r, s2_s, s2_r, y_s, y_r, z_s, z_r, x_s, x_r, p_s, p_r, r_s, r_r, u_s, u_r, b_s, b_r, f_s,
           fz_s, fz_r, fx_s, fx_r, tx_s, tx_r, tz_s, tz_r, in_s, out_s):
    row = lax.axis_index("row")
    col = lax.axis_index("col")
    x, z = col // NZ, col % NZ
    y, core = row // 2, row % 2

    def at_x(d):
        return (row, lax.rem(x + d, NX) * NZ + z)

    def at_z(d):
        return (row, x * NZ + lax.rem(z + d, NZ))

    def at_y(d):
        return (lax.rem(y + d, NY) * 2 + core, col)

    sibling = (y * 2 + 1 - core, col)
    in_slab = col < 2 * NROW

    def shift(r, xs):
        k = lax.rem(r // 2 + 2 * xs, 4)
        return jnp.where(lax.rem(r, 2) == 0, k, jnp.where(k == 0, 4, 8 - k))

    def s2_to(xs):
        return 4 * xs + z // 2, lax.rem(z + shift(row, xs), NZ)

    def s2_self(xs):
        to_row, to_z = s2_to(xs)
        return (to_row == row) & (to_z == z)

    def s2_from(half):
        xs, zs = row // 4, lax.rem(2 * row + half, NZ)
        s = lax.rem(z - zs + NZ, NZ)
        k = lax.rem(jnp.minimum(s, NZ - s) + 2 * xs, 4)
        return 2 * k + (s >= 4).astype(jnp.int32), zs

    def s2_from_self(half):
        r, zs = s2_from(half)
        return (r == row) & (zs == z)

    part = col % 2
    use_col = 2 * row + z // 4
    use_self = use_col == col
    home = in_slab & (col // 2 == row)
    home_y, home_core = (col // 2) // 2, (col // 2) % 2

    def copy(src, dst, ss, rs, dev):
        return pltpu.make_async_remote_copy(src_ref=src, dst_ref=dst, send_sem=ss, recv_sem=rs,
                                            device_id=dev, device_id_type=MESH)

    bar = pltpu.get_barrier_semaphore()

    def greet(dev):
        pl.semaphore_signal(bar, inc=1, device_id=dev, device_id_type=MESH)

    for d in range(1, NZ):
        greet(at_z(d))
    for d in range(1, NX):
        greet(at_x(d))
    for d in range(1, NY):
        greet(at_y(d))
    greet(sibling)
    for half in range(2):
        @pl.when(jnp.logical_not(s2_from_self(half)))
        def _():
            r, zs = s2_from(half)
            greet((r, x * NZ + zs))

    @pl.when(home)
    def _():
        def hello(k, carry):
            xx, zz = k // 4, 4 * part + lax.rem(k, 4)

            @pl.when(xx * NZ + zz != col)
            def _():
                greet((row, xx * NZ + zz))
            return carry

        lax.fori_loop(0, 16, hello, 0)

    loads = [pltpu.make_async_copy(form_hbm, form_ref, in_s.at[0]), pltpu.make_async_copy(born_hbm, born_ref, in_s.at[1])]
    for c in loads:
        c.start()
    for k in range(8):
        sign[k] = jnp.float32((1.0 - 2.0 * (k // 4)) / (1.0 + k % 4))
    colp[:, COLS:, :] = jnp.zeros((NROW, 1024 - COLS, LANE), BF)
    for half in range(2):
        edge = slice(half * PAD + HROW, (half + 1) * PAD)
        zsend[edge, :] = jnp.zeros((PAD - HROW, LANE), BF)
        ssum[edge, :] = jnp.zeros((PAD - HROW, LANE), F32)
        bornp[edge, :] = jnp.zeros((PAD - HROW, LANE), F32)
    t32[:, 60:, :] = jnp.zeros((NX * NZ, 4, LANE), F32)

    n_wait = 7 + 3 + 3 + 1 + 1 - use_self.astype(jnp.int32) + 2
    for xs in range(2):
        n_wait = n_wait - s2_self(xs).astype(jnp.int32)
    pl.semaphore_wait(bar, n_wait)

    def s1_copy(d):
        g = lax.rem(x + d, NX)
        src = rad_ref.at[pl.ds(pl.multiple_of(g * HROW, HROW), HROW)]
        return copy(src, mid.at[x], s1_s.at[d], s1_r.at[x], at_x(d))

    @pl.when(in_slab)
    def _():
        for d in (2, 1, 3):
            s1_copy(d).start()
        mid[x] = rad_ref[pl.ds(pl.multiple_of(x * HROW, HROW), HROW), :]

    below, above = lax.rem(y + 3, NY) * 2 + core, lax.rem(y + 1, NY) * 2 + core
    across = lax.rem(y + 2, NY) * 2 + core
    lo, hi = pl.ds(0, MID), pl.ds(MID, MID)

    def y_copy(k, src, dst, dev):
        return copy(src, dst, y_s.at[k], y_r.at[k], dev)

    def y_part(k, r, part_, dev):
        return y_copy(k, colp.at[r, part_], colp.at[r, part_], dev)

    ys = [
        y_copy(0, rad_ref.at[lo], colp.at[row, lo], at_y(1)),
        y_copy(1, rad_ref.at[hi], colp.at[row, hi], at_y(3)),
        y_copy(2, rad_ref.at[hi], colp.at[row, hi], at_y(1)),
        y_copy(3, rad_ref.at[lo], colp.at[row, lo], at_y(3)),
        y_copy(4, rad_ref, colp.at[row, pl.ds(0, COLS)], sibling),
        y_part(5, below, lo, at_y(1)),
        y_part(6, above, hi, at_y(3)),
        y_part(7, below, lo, sibling),
        y_part(8, above, hi, sibling),
        y_part(9, below, hi, sibling),
        y_part(10, above, lo, sibling),
        y_part(11, across, lo, sibling),
        y_part(12, across, hi, sibling),
    ]
    for k in range(5):
        ys[k].start()
    colp[row, 0:COLS, :] = rad_ref[...]

    def s2_copy(xs):
        to_row, to_z = s2_to(xs)
        half = lax.rem(z, 2)
        return copy(mid.at[xs], rowp.at[x, half, to_z], s2_s.at[xs], s2_r.at[half], (to_row, x * NZ + to_z))

    for xs in range(2):
        @pl.when(x != xs)
        def _():
            copy(mid.at[xs], mid.at[xs], s1_s.at[0], s1_r.at[xs], sibling).wait_recv()

        @pl.when(s2_self(xs))
        def _():
            rowp[x, lax.rem(z, 2), z] = mid[xs]

        @pl.when(jnp.logical_not(s2_self(xs)))
        def _():
            s2_copy(xs).start()

    def flow_at(f):
        if f == 0:
            return x, 0
        return lax.rem(x + f - 1, NX), 1

    def steps(f, sign):
        return 4 if (f <= 2) == (sign > 0) else 3

    def z_copy(f, sign, s):
        g, half = flow_at(f)
        origin = lax.rem(z + (NZ - s if sign > 0 else s), NZ)
        k = (f * 2 + (0 if sign > 0 else 1)) * 4 + s
        ref = rowp.at[g, half, origin]
        return copy(ref, ref, z_s.at[k], z_r.at[k], at_z(1 if sign > 0 else NZ - 1))

    def z_wait(f, sign, s):
        z_copy(f, sign, s).wait_recv()
        if s + 1 < steps(f, sign):
            z_copy(f, sign, s + 1).start()

    def piece(k):
        d = (k + 1) // 2
        return lax.rem(z + (NZ - d if k % 2 == 1 else d), NZ)

    def xh2(k, sign):
        ref = rowp.at[x, 0, piece(k)]
        n = k if sign > 0 else 8 + k
        return copy(ref, ref, x_s.at[n], x_r.at[n], at_x(1 if sign > 0 else 3))

    def xh2_forward(k):
        sign = 1 if k % 2 == 0 else -1
        ref = rowp.at[lax.rem(x + (3 if sign > 0 else 1), NX), 0, piece(k)]
        return copy(ref, ref, x_s.at[16 + k], x_r.at[16 + k], at_x(1 if sign > 0 else 3))

    def xh2_start(k):
        xh2(k, 1).start()
        xh2(k, -1).start()

    def xh2_wait(k):
        xh2(k, 1).wait_recv()
        xh2(k, -1).wait_recv()
        xh2_forward(k).start()

    def xh1(n):
        ref = rowp.at[lax.rem(x + (3 if n == 2 else 0), NX), 1, z]
        return copy(ref, ref, x_s.at[24 + n], x_r.at[24 + n], at_x(3 if n == 1 else 1))

    def flow_start(f):
        z_copy(f, 1, 0).start()
        z_copy(f, -1, 0).start()

    def sc_wait(half):
        @pl.when(jnp.logical_not(s2_from_self(half)))
        def _():
            ref = rowp.at[x, half, z]
            copy(ref, ref, s2_s.at[0], s2_r.at[half], sibling).wait_recv()

    sc_wait(0)
    flow_start(0)
    xh2_start(0)
    sc_wait(1)
    flow_start(1)
    xh1(0).start()
    xh1(1).start()

    def spread(i, carry):
        table[i] = jnp.broadcast_to(form_ref[pl.ds(i, 1), :], (16, GRID)).astype(BF)
        return carry

    def y_on(k, *then):
        ys[k].wait_recv()
        for n in then:
            ys[n].start()

    for c in loads:
        c.wait()
    lax.fori_loop(0, 64, spread, 0, unroll=4)
    y_on(0, 5, 7)
    y_on(1, 6, 8)
    y_on(2, 9)
    y_on(3, 10)
    z_wait(0, 1, 0)
    xh2_start(1)
    z_wait(0, -1, 0)
    xh2_start(2)
    xh1(0).wait_recv()
    xh1(2).start()
    flow_start(4)
    xh1(1).wait_recv()
    flow_start(2)
    xh2_wait(0)
    z_wait(1, 1, 0)
    z_wait(1, -1, 0)
    lax.fori_loop(64, 160, spread, 0, unroll=4)
    z_wait(0, 1, 1)
    xh2_start(3)
    z_wait(0, -1, 1)
    xh2_start(4)
    xh1(2).wait_recv()
    flow_start(3)
    xh2_wait(1)
    xh2_wait(2)
    lax.fori_loop(160, 256, spread, 0, unroll=4)
    for b in range(NB):
        gb_ref[b * MOM:(b + 1) * MOM, :] = jnp.broadcast_to(green_ref[b:b + 1, :], (LANE, MOM)).T
    weighted[...] = (gb_ref[...] * kmat_ref[...].astype(F32)).astype(BF)
    for half in range(2):
        bornp[half * PAD:half * PAD + HROW, :] = born_ref[pl.ds(pl.multiple_of(half * COLS + x * HROW, HROW), HROW), :]
    z_wait(0, 1, 2)
    xh2_start(5)
    z_wait(0, -1, 2)
    xh2_start(6)
    z_wait(1, 1, 1)
    z_wait(1, -1, 1)
    z_wait(0, 1, 3)
    xh2_start(7)
    y_on(5, 11)
    y_on(6, 12)
    for f in (4, 2):
        z_wait(f, 1, 0)
        z_wait(f, -1, 0)
    for k in (4, 7, 8, 9, 10, 11, 12):
        ys[k].wait_recv()

    def before_1():
        z_wait(1, 1, 2)
        z_wait(1, -1, 2)
        xh2_wait(3)
        xh2_wait(4)
        z_wait(3, 1, 0)
        z_wait(3, -1, 0)
        z_wait(1, 1, 3)

    def before_2():
        for f in (4, 2):
            z_wait(f, 1, 1)
            z_wait(f, -1, 1)
        for k in (5, 6, 7):
            xh2_wait(k)

    def before_3():
        z_wait(3, 1, 1)
        z_wait(3, -1, 1)

    def before_4():
        for f in (4, 2):
            z_wait(f, 1, 2)
            z_wait(f, -1, 2)
        for k in range(8):
            xh2_forward(k).wait_recv()

    def before_5():
        z_wait(3, 1, 2)
        z_wait(3, -1, 2)
        z_wait(2, 1, 3)

    def before_6():
        z_wait(4, -1, 3)

    def before_7():
        z_wait(3, -1, 3)

    befores = {1: before_1, 2: before_2, 3: before_3, 4: before_4, 5: before_5, 6: before_6, 7: before_7}

    def p_copy(d, half):
        n = (d - 1) * 2 + half
        return copy(psend.at[n], precv.at[n], p_s.at[n], p_r.at[n], at_x(d))

    def batch(t):
        late = jnp.maximum(t - 2, 0)
        third = lax.rem(late, 3)
        d = jnp.where(t < 2, 0, jnp.where(third == 0, 1, jnp.where(third == 1, 3, 2)))
        half = jnp.where((t == 1) | (t >= 5), 1, 0)
        return d, lax.rem(x + d, NX), half

    lanes = lax.broadcasted_iota(jnp.int32, (MOM, 256), 1)

    def build(t, carry):
        for k, fn in befores.items():
            pl.when(t == k)(fn)
        d, g, half = batch(t)
        first = half * NB + g * HALF
        zs = lax.rem(2 * row + half, NZ)
        slots = [lax.rem(zs + shift(jnp.int32(r), row // 4), NZ) for r in range(NROW)]
        for w in range(NWIN):
            base = w * WIN * MOM
            start = base // LANE * LANE
            off = base - start
            width = min(256, COLS - start)
            win = jnp.concatenate([colp[c, start:start + 256, :] for c in range(8)], axis=1)
            parts = []
            for i in range(HALF):
                chan = jnp.concatenate(
                    [rowp[g, half, slots[c], i * MOM:(i + 1) * MOM, :] for c in range(NROW)], axis=1
                ).reshape(3, 16, GRID)
                for j in range(WIN):
                    factor = table[code_ref[w * WIN + j, first + i] & 255]
                    parts.append((chan * factor[None]).reshape(MOM, GRID))
            scaled = jnp.concatenate(parts, axis=0)
            prod = lax.dot_general(scaled, win, (((1,), (1,)), ((), ())), preferred_element_type=F32)
            for i in range(HALF):
                acc = jnp.zeros((MOM, 256), F32)
                for j in range(WIN):
                    n = i * WIN + j
                    low = off + j * MOM
                    mine = prod[n * MOM:(n + 1) * MOM] * sign[code_ref[w * WIN + j, first + i] >> 8]
                    acc = jnp.where((lanes >= low) & (lanes < low + MOM), mine, acc)
                rows = pl.ds(pl.multiple_of((first + i) * MOM, MOM), MOM)
                new = acc.astype(BF)
                if off:
                    new = jnp.where(lanes >= off, new, vbuf[rows, start:start + width])
                vbuf[rows, start:start + width] = new[:, :width]
        rows = pl.ds(pl.multiple_of(first * MOM, HROW), HROW)
        part_sum = jnp.dot(vbuf[rows, :], weighted[...], preferred_element_type=F32)

        @pl.when(d == 0)
        def _():
            pown[half] = part_sum

        @pl.when(d > 0)
        def _():
            n = (d - 1) * 2 + half
            psend[n] = part_sum.astype(BF)
            p_copy(d, half).start()
        return carry

    lax.fori_loop(0, 8, build, 0)

    def tx_copy(d):
        to = lax.rem(x + d, NX)
        return copy(t16.at[pl.ds(to * NZ, NZ)], txrecv.at[d - 1], tx_s.at[d], tx_r.at[d], at_x(d))

    def second(operand):
        turned = operand.T.astype(BF)

        def chunk(q, carry):
            rows = pl.ds(pl.multiple_of(q * 384, 384), 384)
            prod = lax.dot_general(turned, vbuf[rows, :], (((1,), (1,)), ((), ())), preferred_element_type=F32)
            for jj in range(3):
                pbuf[jj] = prod[:, jj * LANE:(jj + 1) * LANE]
            for jj in range(3):
                for c in range(NX * NZ):
                    t32[c, pl.ds(q * 12 + jj * 4, 4), :] = pbuf[jj, 4 * c:4 * c + 4, :]
            return carry

        lax.fori_loop(0, 5, chunk, 0)
        t16[...] = t32[...].astype(BF)
        for d in (2, 1, 3):
            tx_copy(d).start()

    def turn(m, carry):
        at = pl.ds(pl.multiple_of(m * LANE, LANE), LANE)
        vturn[:, at] = vbuf[at, :].T
        return carry

    @pl.when(jnp.logical_not(in_slab))
    def _():
        second(weighted[...].astype(F32))

    for n in range(6):
        p_copy(n // 2 + 1, n % 2).wait_recv()
    for half in range(2):
        total = pown[half]
        for d in range(3):
            total = total + precv[d * 2 + half].astype(F32)
        ssum[half * PAD:half * PAD + HROW, :] = total
        zsend[half * PAD:half * PAD + HROW, :] = total.astype(BF)

    def shard(q):
        return pl.ds(pl.multiple_of(q * SH, SH), SH)

    def r_copy(d):
        return copy(zsend.at[shard(lax.rem(z + d, NZ))], zrecv.at[d - 1], r_s.at[d], r_r.at[d], at_z(d))

    for d in range(1, NZ):
        r_copy(d).start()
    lax.fori_loop(0, 4, turn, 0)
    for d in range(1, NZ):
        r_copy(d).wait_recv()
    total = bornp[shard(z), :] + ssum[shard(z), :]
    for d in range(NZ - 1):
        total = total + zrecv[d].astype(F32)
    fresh = total.astype(BF)
    fi[x, shard(z), :] = fresh
    def u_copy():
        return copy(fi.at[x, shard(z)], upd.at[x, shard(lax.rem(z, 4))], u_s.at[0], u_r.at[x * 4 + lax.rem(z, 4)],
                    (row, use_col))

    @pl.when(use_self)
    def _():
        upd[x, shard(lax.rem(z, 4)), :] = fresh

    @pl.when(jnp.logical_not(use_self))
    def _():
        u_copy().start()

    def fz_copy(d):
        ref = fi.at[x, shard(z)]
        return copy(ref, ref, fz_s.at[d], fz_r.at[d], at_z(d))

    for d in range(1, NZ):
        fz_copy(d).start()

    def b_copy(d, g):
        ref = upd.at[g, pl.ds(0, HROW)]
        return copy(ref, ref, b_s.at[d * 4 + g], b_r.at[g], sibling if d == 0 else at_y(d))

    def f_copy(g):
        ref = upd.at[g, pl.ds(0, HROW)]
        return copy(ref, ref, f_s.at[g], b_r.at[g], sibling)

    @pl.when(home)
    def _():
        for g in range(NX):
            for q in range(4):
                @pl.when(g * NZ + 4 * part + q != col)
                def _():
                    ref = upd.at[g, pl.ds(q * SH, SH)]
                    copy(ref, ref, u_s.at[0], u_r.at[g * 4 + q], sibling).wait_recv()
            for d in (2, 1, 3, 0):
                b_copy(d, g).start()

    lax.fori_loop(4, 8, turn, 0)
    for d in range(1, NZ):
        ref = fi.at[x, shard(lax.rem(z + NZ - d, NZ))]
        copy(ref, ref, fz_s.at[d], fz_r.at[d], at_z(d)).wait_recv()

    def fx_copy(d, g):
        return copy(fi.at[g], fi.at[g], fx_s.at[d], fx_r.at[d], at_x(d))

    for d in (2, 1, 3):
        fx_copy(d, x).start()

    @pl.when(in_slab)
    def _():
        @pl.when(jnp.logical_not(home))
        def _():
            for g in range(NX):
                f_copy(g).wait_recv()

                @pl.when((core == home_core) & (y != home_y))
                def _():
                    f_copy(g).start()
        fresh_rows = jnp.concatenate([upd[g, 0:HROW, :] for g in range(NX)], axis=0)
        second((gb_ref[...] * fresh_rows.astype(F32)).astype(BF).astype(F32))

    lax.fori_loop(8, 15, turn, 0)

    def v_copy():
        return pltpu.make_async_copy(vturn, v_out, out_s.at[8])

    v_copy().start()
    for j in range(15):
        bturn[j] = born_ref[j * LANE:(j + 1) * LANE, :].T

    for d in range(1, NX):
        tx_copy(d).wait_recv()
    total = t32[pl.ds(x * NZ, NZ)]
    for d in range(NX - 1):
        total = total + txrecv[d].astype(F32)
    tz32[...] = total
    tzsend[...] = total.astype(BF)

    def tz_copy(d):
        return copy(tzsend.at[lax.rem(z + d, NZ)], tzrecv.at[d - 1], tz_s.at[d], tz_r.at[d], at_z(d))

    for d in range(1, NZ):
        tz_copy(d).start()
    for d in range(1, NX):
        fx_copy(d, lax.rem(x + NX - d, NX)).wait_recv()

    def f_out(g, half):
        return pltpu.make_async_copy(fi.at[g, pl.ds(half * PAD, HROW)],
                                     first_out.at[pl.ds(half * COLS + g * HROW, HROW)], out_s.at[2 * g + half])

    for g in range(NX):
        for half in range(2):
            f_out(g, half).start()
    for d in range(1, NZ):
        tz_copy(d).wait_recv()
    total = tz32[z]
    for d in range(NZ - 1):
        total = total + tzrecv[d].astype(F32)
    tz32[z] = total
    for j in range(15):
        share_out[:, j * LANE:(j + 1) * LANE] = tz32[z, 4 * j:4 * j + 4, :] + bturn[j, pl.ds(4 * col, 4), :]

    for g in range(NX):
        for half in range(2):
            f_out(g, half).wait()
    v_copy().wait()

    @pl.when(in_slab)
    def _():
        for d in range(1, NX):
            s1_copy(d).wait_send()

    for xs in range(2):
        @pl.when(jnp.logical_not(s2_self(xs)))
        def _():
            s2_copy(xs).wait_send()
    for c in ys:
        c.wait_send()
    for f in range(5):
        for sign in (1, -1):
            for s in range(steps(f, sign)):
                z_copy(f, sign, s).wait_send()
    for k in range(8):
        xh2(k, 1).wait_send()
        xh2(k, -1).wait_send()
        xh2_forward(k).wait_send()
    for n in range(3):
        xh1(n).wait_send()
    for n in range(6):
        p_copy(n // 2 + 1, n % 2).wait_send()
    for d in range(1, NZ):
        r_copy(d).wait_send()
        fz_copy(d).wait_send()
        tz_copy(d).wait_send()
    for d in range(1, NX):
        fx_copy(d, x).wait_send()
        tx_copy(d).wait_send()

    @pl.when(jnp.logical_not(use_self))
    def _():
        u_copy().wait_send()

    @pl.when(home)
    def _():
        for g in range(NX):
            for d in range(4):
                b_copy(d, g).wait_send()

    @pl.when(in_slab & jnp.logical_not(home) & (core == home_core) & (y != home_y))
    def _():
        for g in range(NX):
            f_copy(g).wait_send()


def body(radial, form_factors, coupling, quantum, green_diag, kmatrix, born_term):
    row_count, col_count = coupling.shape
    row_index, col_index = lax.axis_index("row"), lax.axis_index("col")
    rq = lax.dynamic_slice_in_dim(quantum, row_index * row_count, row_count, 0)
    cq = lax.dynamic_slice_in_dim(quantum, col_index * col_count, col_count, 0)
    table_index = coupling * (NTARG * NTARG) + rq[:, 2:3] * NTARG + cq[:, 2][None, :]
    parity = (rq[:, 0:1] + cq[:, 0][None, :]) % 2
    spread_m = jnp.abs(rq[:, 1:2] - cq[:, 1][None, :])
    code = (table_index + 256 * (4 * parity + spread_m)).T
    vm = pl.BlockSpec(memory_space=pltpu.VMEM)
    sm = pl.BlockSpec(memory_space=pltpu.SMEM)
    hb = pl.BlockSpec(memory_space=pl.ANY)
    dma = pltpu.SemaphoreType.DMA
    v_block, first, share = pl.pallas_call(
        kernel,
        out_shape=(
            jax.ShapeDtypeStruct((COLS, ROWS), BF),
            jax.ShapeDtypeStruct((ROWS, LANE), BF),
            jax.ShapeDtypeStruct((4, ROWS), F32),
        ),
        in_specs=[sm, vm, hb, vm, vm, hb],
        out_specs=(hb, hb, vm),
        scratch_shapes=[
            pltpu.SMEM((8,), F32),
            pltpu.VMEM((256, 16, GRID), BF),
            pltpu.VMEM((256, GRID), F32),
            pltpu.VMEM((NROW, 1024, LANE), BF),
            pltpu.VMEM((NX, 2, NROW, HROW, LANE), BF),
            pltpu.VMEM((2, HROW, LANE), BF),
            pltpu.VMEM((ROWS, COLS), BF),
            pltpu.VMEM((COLS, ROWS), BF),
            pltpu.VMEM((COLS, LANE), F32),
            pltpu.VMEM((COLS, LANE), BF),
            pltpu.VMEM((2, HROW, LANE), F32),
            pltpu.VMEM((6, HROW, LANE), BF),
            pltpu.VMEM((6, HROW, LANE), BF),
            pltpu.VMEM((2 * PAD, LANE), F32),
            pltpu.VMEM((2 * PAD, LANE), BF),
            pltpu.VMEM((NZ - 1, SH, LANE), BF),
            pltpu.VMEM((ROWS, LANE), F32),
            pltpu.VMEM((2 * PAD, LANE), F32),
            pltpu.VMEM((15, LANE, LANE), F32),
            pltpu.VMEM((NX, 2 * PAD, LANE), BF),
            pltpu.VMEM((NX, PAD, LANE), BF),
            pltpu.VMEM((NX * NZ, SH, LANE), F32),
            pltpu.VMEM((NX * NZ, SH, LANE), BF),
            pltpu.VMEM((3, LANE, LANE), F32),
            pltpu.VMEM((NX - 1, NZ, SH, LANE), BF),
            pltpu.VMEM((NZ, SH, LANE), F32),
            pltpu.VMEM((NZ, SH, LANE), BF),
            pltpu.VMEM((NZ - 1, SH, LANE), BF),
            dma((4,)), dma((2,)), dma((2,)), dma((2,)), dma((13,)), dma((13,)), dma((40,)), dma((40,)), dma((27,)), dma((27,)),
            dma((6,)), dma((6,)), dma((8,)), dma((8,)), dma((1,)), dma((16,)), dma((16,)), dma((4,)), dma((4,)),
            dma((8,)), dma((8,)), dma((4,)), dma((4,)), dma((4,)), dma((4,)), dma((8,)), dma((8,)), dma((2,)), dma((9,)),
        ],
        compiler_params=pltpu.CompilerParams(collective_id=0, has_side_effects=True, vmem_limit_bytes=58 << 20),
        name="sweeps",
    )(code, radial.reshape(COLS, LANE), form_factors, green_diag, kmatrix, born_term)
    return v_block.T, first, share.T


def solution(mesh):
    placed = (
        P("col", None, "row"),
        P(),
        P("row", "col"),
        P(),
        P("col", None),
        P("col", None),
        P("row", None),
    )
    return jax.shard_map(
        body,
        mesh=mesh,
        in_specs=placed,
        out_specs=(P("row", "col"), P("row", None), P("row", "col")),
        check_vma=False,
    )
```

time: 147 us -> 119 us (0.81)
  Pallas kernels: 131 us -> 110 us
  local copies, waits for them, and re-layouts: 11.2 us -> 6.44 us
    pallas_call x1, Pallas kernels: 131 us -> 110 us  [body(): pl.pallas_call(kernel, out_shape=(jax.ShapeDtypeStruct((COLS, ROWS), BF),...]
    unnamed x12 -> x9, local copies, waits for them, and re-layouts: 8.91 us -> 6.29 us
    broadcast_in_dim x2 -> x0, local copies, waits for them, and re-layouts: 1.76 us -> none  [body(): green = jnp.broadcast_to(green_diag.reshape(COLS, 1), (COLS, LANE))]
where the time goes in v2:
time: 119 us
  Pallas kernels  110 us (92%)
  local copies, waits for them, and re-layouts  6.44 us (5%)
  other arithmetic  1.4 us (1%)
    pallas_call x1, Pallas kernels, body(): pl.pallas_call(kernel, out_shape=(jax.ShapeDtypeStruct((COLS, ROWS), BF),...  110 us
    unnamed x9, local copies, waits for them, and re-layouts  6.29 us

profile of v2, /device:TPU:1, one launch (start us, length us, event | category | flops | bytes accessed | tf_op | source)
XLA Modules:
  0.0 118.5 jit_solution(15582742749534530321)
XLA Ops:
  0.6 0.0 copy-start
  0.7 0.7 copy-done
  1.3 0.1 constant_dynamic-slice_fusion
  1.4 0.1 constant_dynamic-slice_fusion.1
  1.5 1.4 %fusion.4.code_ref = s32[20,40]{1,0:T(8,128)} fusion(s32[40,20]{0,1:T(8,128)} %param.9, s32[20]{0:T(128)S(1)} %get-tuple-element.13, s32[40]{0:T(128)S(1)} %get-tuple-element.10, s32[20]{0:T(128)S(1)} %get-tuple-element.14, s32[40]{0:T(128)S(1)} %get-tuple-element.11, s32[20]{0:T(128)S(1)} %get-tuple-element.12, s32[40]{0:T(128)S(1)} %get-tuple-element.9), kind=kLoop, calls=%fused_computation.9 | loop fusion | flops 16800 | bytes 7120 | tf_op jit(solution)/shard_map/transpose | solution.py:638
  2.9 110.0 %sweeps.1 = (bf16[960,1920]{1,0:T(8,128)(2,1)}, bf16[1920,128]{1,0:T(8,128)(2,1)}, f32[4,1920]{1,0:T(4,128)}) custom-call(s32[20,40]{1,0:T(8,128)} %fusion.4.code_ref, bf16[960,128]{1,0:T(8,128)(2,1)} %bitcast.18, f32[256,1024]{1,0:T(8,128)} %form_hbm.1, f32[20,48]{1,0:T(8,128)} %green_ref.1, bf16[960,128]{1,0:T(8,128)(2,1)} %kmat_ref.1, f32[1920,128]{1,0:T(8,128)} %born_hbm.1), custom_call_target="tpu_custom_call" | custom-call | tf_op jit(solution)/shard_map/sweeps/pallas_call | solution.py:643
  112.9 0.0 copy-start.1
  112.9 0.0 copy-start.2
  112.9 4.2 %copy.13 = bf16[1920,960]{0,1:T(8,128)(2,1)} copy(bf16[1920,960]{0,1:T(8,128)(2,1)} %bitcast.17) | data formatting | bytes 7372800
  117.1 0.0 copy-done.1
  117.1 0.8 copy.14
  117.9 0.0 copy-done.2
  117.9 0.6 copy.15
  (2 shorter events, 0.0 us)
Async XLA Ops:
  0.6 0.7 copy-start
  112.9 4.2 %copy-start.1 = (bf16[1920,128]{1,0:T(8,128)(2,1)S(1)}, bf16[1920,128]{1,0:T(8,128)(2,1)}, u32[]{:S(2)}) copy-start(bf16[1920,128]{1,0:T(8,128)(2,1)} %get-tuple-element.19) | copy-start | bytes 1474564
  112.9 5.0 %copy-start.2 = (f32[4,1920]{1,0:T(4,128)S(1)}, f32[4,1920]{1,0:T(4,128)}, u32[]{:S(2)}) copy-start(f32[4,1920]{1,0:T(4,128)} %get-tuple-element.8) | copy-start | bytes 92164

commit v3 on v2

--- a/solution.py
+++ b/solution.py
@@ -31,8 +31,8 @@
 def kernel(code_ref, rad_ref, form_hbm, green_ref, kmat_ref, born_hbm,
            v_out, first_out, share_out,
            sign, table, form_ref, colp, rowp, mid, vbuf, vturn, gb_ref, weighted, pown, psend, precv, ssum, zsend, zrecv,
-           born_ref, bornp, bturn, fi, upd, t32, t16, pbuf, txrecv, tz32, tzsend, tzrecv,
-           s1_s, s1_r, s2_s, s2_r, y_s, y_r, z_s, z_r, x_s, x_r, p_s, p_r, r_s, r_r, u_s, u_r, b_s, b_r, f_s,
+           born_ref, bornp, bturn, vsum, fi, yshard, upd, t32, t16, pbuf, txrecv, tz32, tzsend, tzrecv,
+           s1_s, s1_r, s2_s, s2_r, y_s, y_r, z_s, z_r, x_s, x_r, p_s, p_r, r_s, r_r, a_s, a_r, u_s, u_r, f_s, f_r,
            fz_s, fz_r, fx_s, fx_r, tx_s, tx_r, tz_s, tz_r, in_s, out_s):
     row = lax.axis_index("row")
     col = lax.axis_index("col")
@@ -73,14 +73,19 @@
         return (r == row) & (zs == z)
 
     part = col % 2
-    use_col = 2 * row + z // 4
-    use_self = use_col == col
-    home = in_slab & (col // 2 == row)
-    home_y, home_core = (col // 2) // 2, (col // 2) % 2
+
+    def use_col(from_y):
+        return from_y // 2 * NZ + 4 * lax.rem(from_y, 2) + 2 * core + z // 4
+
+    home = in_slab & ((col // 2) % 2 == core)
 
     def copy(src, dst, ss, rs, dev):
         return pltpu.make_async_remote_copy(src_ref=src, dst_ref=dst, send_sem=ss, recv_sem=rs,
                                             device_id=dev, device_id_type=MESH)
+
+    loads = [pltpu.make_async_copy(form_hbm, form_ref, in_s.at[0]), pltpu.make_async_copy(born_hbm, born_ref, in_s.at[1])]
+    for c in loads:
+        c.start()
 
     bar = pltpu.get_barrier_semaphore()
 
@@ -112,9 +117,6 @@
 
         lax.fori_loop(0, 16, hello, 0)
 
-    loads = [pltpu.make_async_copy(form_hbm, form_ref, in_s.at[0]), pltpu.make_async_copy(born_hbm, born_ref, in_s.at[1])]
-    for c in loads:
-        c.start()
     for k in range(8):
         sign[k] = jnp.float32((1.0 - 2.0 * (k // 4)) / (1.0 + k % 4))
     colp[:, COLS:, :] = jnp.zeros((NROW, 1024 - COLS, LANE), BF)
@@ -125,7 +127,20 @@
         bornp[edge, :] = jnp.zeros((PAD - HROW, LANE), F32)
     t32[:, 60:, :] = jnp.zeros((NX * NZ, 4, LANE), F32)
 
-    n_wait = 7 + 3 + 3 + 1 + 1 - use_self.astype(jnp.int32) + 2
+    for b in range(NB):
+        gb_ref[b * MOM:(b + 1) * MOM, :] = jnp.broadcast_to(green_ref[b:b + 1, :], (LANE, MOM)).T
+    weighted[...] = (gb_ref[...] * kmat_ref[...].astype(F32)).astype(BF)
+
+    def spread(i, carry):
+        table[i] = jnp.broadcast_to(form_ref[pl.ds(i, 1), :], (16, GRID)).astype(BF)
+        return carry
+
+    loads[0].wait()
+    lax.fori_loop(0, 128, spread, 0, unroll=4)
+
+    n_wait = 7 + 3 + 3 + 1 + 4 + 2
+    for from_y in range(NY):
+        n_wait = n_wait - (use_col(from_y) == col).astype(jnp.int32)
     for xs in range(2):
         n_wait = n_wait - s2_self(xs).astype(jnp.int32)
     pl.semaphore_wait(bar, n_wait)
@@ -253,96 +268,83 @@
     xh1(0).start()
     xh1(1).start()
 
-    def spread(i, carry):
-        table[i] = jnp.broadcast_to(form_ref[pl.ds(i, 1), :], (16, GRID)).astype(BF)
-        return carry
-
     def y_on(k, *then):
         ys[k].wait_recv()
         for n in then:
             ys[n].start()
 
-    for c in loads:
-        c.wait()
-    lax.fori_loop(0, 64, spread, 0, unroll=4)
     y_on(0, 5, 7)
     y_on(1, 6, 8)
+    lax.fori_loop(128, 192, spread, 0, unroll=4)
     y_on(2, 9)
     y_on(3, 10)
-    z_wait(0, 1, 0)
-    xh2_start(1)
-    z_wait(0, -1, 0)
-    xh2_start(2)
-    xh1(0).wait_recv()
-    xh1(2).start()
-    flow_start(4)
-    xh1(1).wait_recv()
-    flow_start(2)
-    xh2_wait(0)
-    z_wait(1, 1, 0)
-    z_wait(1, -1, 0)
-    lax.fori_loop(64, 160, spread, 0, unroll=4)
-    z_wait(0, 1, 1)
-    xh2_start(3)
-    z_wait(0, -1, 1)
-    xh2_start(4)
-    xh1(2).wait_recv()
-    flow_start(3)
-    xh2_wait(1)
-    xh2_wait(2)
-    lax.fori_loop(160, 256, spread, 0, unroll=4)
-    for b in range(NB):
-        gb_ref[b * MOM:(b + 1) * MOM, :] = jnp.broadcast_to(green_ref[b:b + 1, :], (LANE, MOM)).T
-    weighted[...] = (gb_ref[...] * kmat_ref[...].astype(F32)).astype(BF)
-    for half in range(2):
-        bornp[half * PAD:half * PAD + HROW, :] = born_ref[pl.ds(pl.multiple_of(half * COLS + x * HROW, HROW), HROW), :]
-    z_wait(0, 1, 2)
-    xh2_start(5)
-    z_wait(0, -1, 2)
-    xh2_start(6)
-    z_wait(1, 1, 1)
-    z_wait(1, -1, 1)
-    z_wait(0, 1, 3)
-    xh2_start(7)
-    y_on(5, 11)
-    y_on(6, 12)
-    for f in (4, 2):
-        z_wait(f, 1, 0)
-        z_wait(f, -1, 0)
-    for k in (4, 7, 8, 9, 10, 11, 12):
-        ys[k].wait_recv()
-
-    def before_1():
-        z_wait(1, 1, 2)
-        z_wait(1, -1, 2)
+
+    def own_step(s_):
+        for sign_ in (1, -1):
+            if s_ < steps(0, sign_):
+                z_wait(0, sign_, s_)
+                xh2_start(2 * s_ + (1 if sign_ > 0 else 2))
+        for sign_ in (1, -1):
+            if s_ < steps(1, sign_):
+                z_wait(1, sign_, s_)
+
+    def others(s_, *flows):
+        for f in flows:
+            for sign_ in (1, -1):
+                if s_ < steps(f, sign_):
+                    z_wait(f, sign_, s_)
+
+    def part_0():
+        own_step(0)
+        lax.fori_loop(192, 256, spread, 0, unroll=4)
+        y_on(5, 11)
+        y_on(6, 12)
+        xh1(0).wait_recv()
+        xh1(2).start()
+        flow_start(4)
+        xh1(1).wait_recv()
+        flow_start(2)
+        xh2_wait(0)
+        for k in (4, 7, 8, 9, 10, 11, 12):
+            ys[k].wait_recv()
+
+    def part_1():
+        own_step(1)
+        xh1(2).wait_recv()
+        flow_start(3)
+        others(0, 4, 2)
+        xh2_wait(1)
+        xh2_wait(2)
+
+    def part_2():
+        own_step(2)
         xh2_wait(3)
         xh2_wait(4)
-        z_wait(3, 1, 0)
-        z_wait(3, -1, 0)
-        z_wait(1, 1, 3)
+        loads[1].wait()
+        for half in range(2):
+            bornp[half * PAD:half * PAD + HROW, :] = born_ref[pl.ds(pl.multiple_of(half * COLS + x * HROW, HROW), HROW), :]
+
+    def part_3():
+        own_step(3)
+        others(1, 4, 2)
+        others(0, 3)
+        xh2_wait(5)
+        xh2_wait(6)
 
     def before_2():
-        for f in (4, 2):
-            z_wait(f, 1, 1)
-            z_wait(f, -1, 1)
-        for k in (5, 6, 7):
-            xh2_wait(k)
+        xh2_wait(7)
 
     def before_3():
-        z_wait(3, 1, 1)
-        z_wait(3, -1, 1)
+        others(2, 4, 2)
+        others(1, 3)
 
     def before_4():
-        for f in (4, 2):
-            z_wait(f, 1, 2)
-            z_wait(f, -1, 2)
         for k in range(8):
             xh2_forward(k).wait_recv()
 
     def before_5():
-        z_wait(3, 1, 2)
-        z_wait(3, -1, 2)
         z_wait(2, 1, 3)
+        others(2, 3)
 
     def before_6():
         z_wait(4, -1, 3)
@@ -350,42 +352,45 @@
     def before_7():
         z_wait(3, -1, 3)
 
-    befores = {1: before_1, 2: before_2, 3: before_3, 4: before_4, 5: before_5, 6: before_6, 7: before_7}
+    parts_before = {0: part_0, 1: part_1, 2: part_2, 3: part_3}
+    befores = {2: before_2, 3: before_3, 4: before_4, 5: before_5, 6: before_6, 7: before_7}
 
     def p_copy(d, half):
         n = (d - 1) * 2 + half
         return copy(psend.at[n], precv.at[n], p_s.at[n], p_r.at[n], at_x(d))
 
     def batch(t):
-        late = jnp.maximum(t - 2, 0)
-        third = lax.rem(late, 3)
-        d = jnp.where(t < 2, 0, jnp.where(third == 0, 1, jnp.where(third == 1, 3, 2)))
-        half = jnp.where((t == 1) | (t >= 5), 1, 0)
+        third = lax.rem(t - 2, 3)
+        d = jnp.where(third == 0, 1, jnp.where(third == 1, 3, 2))
+        half = jnp.where(t >= 5, 1, 0)
         return d, lax.rem(x + d, NX), half
 
     lanes = lax.broadcasted_iota(jnp.int32, (MOM, 256), 1)
 
-    def build(t, carry):
-        for k, fn in befores.items():
-            pl.when(t == k)(fn)
-        d, g, half = batch(t)
+    def grid_part(half, slot_):
+        step = lax.rem(slot_ - lax.rem(2 * row + half, NZ) + NZ, NZ)
+        k = lax.rem(jnp.minimum(step, NZ - step) + 2 * (row // 4), 4)
+        return 2 * k + (step >= 4).astype(jnp.int32)
+
+    def products(g, half, chunks, put):
         first = half * NB + g * HALF
-        zs = lax.rem(2 * row + half, NZ)
-        slots = [lax.rem(zs + shift(jnp.int32(r), row // 4), NZ) for r in range(NROW)]
         for w in range(NWIN):
             base = w * WIN * MOM
             start = base // LANE * LANE
             off = base - start
-            width = min(256, COLS - start)
-            win = jnp.concatenate([colp[c, start:start + 256, :] for c in range(8)], axis=1)
+            win = jnp.concatenate([colp[r, start:start + 256, :] for _, r in chunks], axis=1)
             parts = []
             for i in range(HALF):
-                chan = jnp.concatenate(
-                    [rowp[g, half, slots[c], i * MOM:(i + 1) * MOM, :] for c in range(NROW)], axis=1
-                ).reshape(3, 16, GRID)
+                chan = jnp.concatenate([rowp[g, half, c, i * MOM:(i + 1) * MOM, :] for c, _ in chunks], axis=1)
+                chan = chan.reshape(3, 16, len(chunks) * LANE)
                 for j in range(WIN):
-                    factor = table[code_ref[w * WIN + j, first + i] & 255]
-                    parts.append((chan * factor[None]).reshape(MOM, GRID))
+                    which = code_ref[w * WIN + j, first + i] & 255
+                    if len(chunks) == NROW:
+                        factor = table[which]
+                    else:
+                        factor = jnp.concatenate(
+                            [table[which, :, pl.ds(pl.multiple_of(r * LANE, LANE), LANE)] for _, r in chunks], axis=1)
+                    parts.append((chan * factor[None]).reshape(MOM, len(chunks) * LANE))
             scaled = jnp.concatenate(parts, axis=0)
             prod = lax.dot_general(scaled, win, (((1,), (1,)), ((), ())), preferred_element_type=F32)
             for i in range(HALF):
@@ -395,26 +400,61 @@
                     low = off + j * MOM
                     mine = prod[n * MOM:(n + 1) * MOM] * sign[code_ref[w * WIN + j, first + i] >> 8]
                     acc = jnp.where((lanes >= low) & (lanes < low + MOM), mine, acc)
-                rows = pl.ds(pl.multiple_of((first + i) * MOM, MOM), MOM)
-                new = acc.astype(BF)
-                if off:
-                    new = jnp.where(lanes >= off, new, vbuf[rows, start:start + width])
-                vbuf[rows, start:start + width] = new[:, :width]
-        rows = pl.ds(pl.multiple_of(first * MOM, HROW), HROW)
-        part_sum = jnp.dot(vbuf[rows, :], weighted[...], preferred_element_type=F32)
-
-        @pl.when(d == 0)
-        def _():
-            pown[half] = part_sum
-
-        @pl.when(d > 0)
-        def _():
-            n = (d - 1) * 2 + half
-            psend[n] = part_sum.astype(BF)
-            p_copy(d, half).start()
+                put(i, start, off, acc)
+
+    def batch_rows(g, half):
+        return pl.ds(pl.multiple_of((half * NB + g * HALF) * MOM, HROW), HROW)
+
+    vsum[...] = jnp.zeros((2, HROW, 1024), F32)
+
+    def own_part(p, carry):
+        for k, fn in parts_before.items():
+            pl.when(p == k)(fn)
+
+        def place(k):
+            d = (k + 1) // 2
+            return lax.rem(jnp.where(lax.rem(k, 2) == 1, z + NZ - d, z + d), NZ)
+
+        def one(half, carry_):
+            chunks = []
+            for k in (2 * p, 2 * p + 1):
+                chunks.append((place(k), grid_part(half, place(k))))
+
+            def put(i, start, off, acc):
+                vsum[half, i * MOM:(i + 1) * MOM, start:start + 256] += acc
+
+            products(x, half, chunks, put)
+            return carry_
+
+        return lax.fori_loop(0, 2, one, carry)
+
+    lax.fori_loop(0, 4, own_part, 0)
+    for half in range(2):
+        vbuf[batch_rows(x, half), :] = vsum[half, :, 0:COLS].astype(BF)
+        pown[half] = jnp.dot(vbuf[batch_rows(x, half), :], weighted[...], preferred_element_type=F32)
+
+    def build(t, carry):
+        for k, fn in befores.items():
+            pl.when(t == k)(fn)
+        d, g, half = batch(t)
+        zs = lax.rem(2 * row + half, NZ)
+        chunks = [(lax.rem(zs + shift(jnp.int32(r), row // 4), NZ), r) for r in range(NROW)]
+
+        def put(i, start, off, acc):
+            rows = pl.ds(pl.multiple_of((half * NB + g * HALF + i) * MOM, MOM), MOM)
+            width = min(256, COLS - start)
+            new = acc.astype(BF)
+            if off:
+                new = jnp.where(lanes >= off, new, vbuf[rows, start:start + width])
+            vbuf[rows, start:start + width] = new[:, :width]
+
+        products(g, half, chunks, put)
+        part_sum = jnp.dot(vbuf[batch_rows(g, half), :], weighted[...], preferred_element_type=F32)
+        psend[(d - 1) * 2 + half] = part_sum.astype(BF)
+        p_copy(d, half).start()
         return carry
 
-    lax.fori_loop(0, 8, build, 0)
+    lax.fori_loop(2, 8, build, 0)
 
     def tx_copy(d):
         to = lax.rem(x + d, NX)
@@ -472,17 +512,34 @@
         total = total + zrecv[d].astype(F32)
     fresh = total.astype(BF)
     fi[x, shard(z), :] = fresh
-    def u_copy():
-        return copy(fi.at[x, shard(z)], upd.at[x, shard(lax.rem(z, 4))], u_s.at[0], u_r.at[x * 4 + lax.rem(z, 4)],
-                    (row, use_col))
-
-    @pl.when(use_self)
-    def _():
-        upd[x, shard(lax.rem(z, 4)), :] = fresh
-
-    @pl.when(jnp.logical_not(use_self))
-    def _():
-        u_copy().start()
+    yshard[y] = fresh
+
+    def a_copy(d):
+        return copy(yshard.at[y], yshard.at[y], a_s.at[d], a_r.at[d], at_y(d))
+
+    for d in (2, 1, 3):
+        a_copy(d).start()
+
+    def u_copy(d):
+        from_y = lax.rem(y + d, NY)
+        return copy(yshard.at[from_y], upd.at[x, shard(lax.rem(z, 4))], u_s.at[d], u_r.at[x * 4 + lax.rem(z, 4)],
+                    (row, use_col(from_y)))
+
+    def u_self(d):
+        return use_col(lax.rem(y + d, NY)) == col
+
+    for d in (0, 1, 3, 2):
+        if d > 0:
+            from_y = lax.rem(y + d, NY)
+            copy(yshard.at[from_y], yshard.at[from_y], a_s.at[d], a_r.at[NY - d], at_y(d)).wait_recv()
+
+        @pl.when(u_self(d))
+        def _():
+            upd[x, shard(lax.rem(z, 4)), :] = yshard[lax.rem(y + d, NY)]
+
+        @pl.when(jnp.logical_not(u_self(d)))
+        def _():
+            u_copy(d).start()
 
     def fz_copy(d):
         ref = fi.at[x, shard(z)]
@@ -491,13 +548,11 @@
     for d in range(1, NZ):
         fz_copy(d).start()
 
-    def b_copy(d, g):
-        ref = upd.at[g, pl.ds(0, HROW)]
-        return copy(ref, ref, b_s.at[d * 4 + g], b_r.at[g], sibling if d == 0 else at_y(d))
-
     def f_copy(g):
         ref = upd.at[g, pl.ds(0, HROW)]
-        return copy(ref, ref, f_s.at[g], b_r.at[g], sibling)
+        return copy(ref, ref, f_s.at[g], f_r.at[g], sibling)
+
+    lax.fori_loop(4, 8, turn, 0)
 
     @pl.when(home)
     def _():
@@ -507,10 +562,17 @@
                 def _():
                     ref = upd.at[g, pl.ds(q * SH, SH)]
                     copy(ref, ref, u_s.at[0], u_r.at[g * 4 + q], sibling).wait_recv()
-            for d in (2, 1, 3, 0):
-                b_copy(d, g).start()
-
-    lax.fori_loop(4, 8, turn, 0)
+            f_copy(g).start()
+
+    @pl.when(in_slab)
+    def _():
+        @pl.when(jnp.logical_not(home))
+        def _():
+            for g in range(NX):
+                f_copy(g).wait_recv()
+        fresh_rows = jnp.concatenate([upd[g, 0:HROW, :] for g in range(NX)], axis=0)
+        second((gb_ref[...] * fresh_rows.astype(F32)).astype(BF).astype(F32))
+
     for d in range(1, NZ):
         ref = fi.at[x, shard(lax.rem(z + NZ - d, NZ))]
         copy(ref, ref, fz_s.at[d], fz_r.at[d], at_z(d)).wait_recv()
@@ -520,19 +582,6 @@
 
     for d in (2, 1, 3):
         fx_copy(d, x).start()
-
-    @pl.when(in_slab)
-    def _():
-        @pl.when(jnp.logical_not(home))
-        def _():
-            for g in range(NX):
-                f_copy(g).wait_recv()
-
-                @pl.when((core == home_core) & (y != home_y))
-                def _():
-                    f_copy(g).start()
-        fresh_rows = jnp.concatenate([upd[g, 0:HROW, :] for g in range(NX)], axis=0)
-        second((gb_ref[...] * fresh_rows.astype(F32)).astype(BF).astype(F32))
 
     lax.fori_loop(8, 15, turn, 0)
 
@@ -611,20 +660,33 @@
         fx_copy(d, x).wait_send()
         tx_copy(d).wait_send()
 
-    @pl.when(jnp.logical_not(use_self))
-    def _():
-        u_copy().wait_send()
+    for d in range(1, NY):
+        a_copy(d).wait_send()
+    for d in range(NY):
+        @pl.when(jnp.logical_not(u_self(d)))
+        def _():
+            u_copy(d).wait_send()
 
     @pl.when(home)
     def _():
         for g in range(NX):
-            for d in range(4):
-                b_copy(d, g).wait_send()
-
-    @pl.when(in_slab & jnp.logical_not(home) & (core == home_core) & (y != home_y))
-    def _():
-        for g in range(NX):
             f_copy(g).wait_send()
+
+
+def hand_over(v_in, f_in, s_in, v_out, f_out, s_out, v_mid, f_mid, s_mid, sem):
+    trips = [(f_in, f_mid, f_out), (s_in, s_mid, s_out)]
+    for q in range(6):
+        rows = pl.ds(q * 160, 160)
+        trips.append((v_in.at[rows], v_mid.at[rows], v_out.at[rows]))
+    there = [pltpu.make_async_copy(src, mid, sem.at[n]) for n, (src, mid, _) in enumerate(trips)]
+    back = [pltpu.make_async_copy(mid, dst, sem.at[8 + n]) for n, (_, mid, dst) in enumerate(trips)]
+    for c in there:
+        c.start()
+    for c, d in zip(there, back):
+        c.wait()
+        d.start()
+    for c in back:
+        c.wait()
 
 
 def body(radial, form_factors, coupling, quantum, green_diag, kmatrix, born_term):
@@ -669,7 +731,9 @@
             pltpu.VMEM((ROWS, LANE), F32),
             pltpu.VMEM((2 * PAD, LANE), F32),
             pltpu.VMEM((15, LANE, LANE), F32),
+            pltpu.VMEM((2, HROW, 1024), F32),
             pltpu.VMEM((NX, 2 * PAD, LANE), BF),
+            pltpu.VMEM((NY, SH, LANE), BF),
             pltpu.VMEM((NX, PAD, LANE), BF),
             pltpu.VMEM((NX * NZ, SH, LANE), F32),
             pltpu.VMEM((NX * NZ, SH, LANE), BF),
@@ -679,12 +743,24 @@
             pltpu.VMEM((NZ, SH, LANE), BF),
             pltpu.VMEM((NZ - 1, SH, LANE), BF),
             dma((4,)), dma((2,)), dma((2,)), dma((2,)), dma((13,)), dma((13,)), dma((40,)), dma((40,)), dma((27,)), dma((27,)),
-            dma((6,)), dma((6,)), dma((8,)), dma((8,)), dma((1,)), dma((16,)), dma((16,)), dma((4,)), dma((4,)),
+            dma((6,)), dma((6,)), dma((8,)), dma((8,)), dma((4,)), dma((4,)), dma((4,)), dma((16,)), dma((4,)), dma((4,)),
             dma((8,)), dma((8,)), dma((4,)), dma((4,)), dma((4,)), dma((4,)), dma((8,)), dma((8,)), dma((2,)), dma((9,)),
         ],
         compiler_params=pltpu.CompilerParams(collective_id=0, has_side_effects=True, vmem_limit_bytes=58 << 20),
         name="sweeps",
     )(code, radial.reshape(COLS, LANE), form_factors, green_diag, kmatrix, born_term)
+    v_block, first, share = pl.pallas_call(
+        hand_over,
+        out_shape=(
+            jax.ShapeDtypeStruct((COLS, ROWS), BF),
+            jax.ShapeDtypeStruct((ROWS, LANE), BF),
+            jax.ShapeDtypeStruct((4, ROWS), F32),
+        ),
+        in_specs=[hb, hb, hb],
+        out_specs=(hb, hb, hb),
+        scratch_shapes=[pltpu.VMEM((COLS, ROWS), BF), pltpu.VMEM((ROWS, LANE), BF), pltpu.VMEM((4, ROWS), F32), dma((16,))],
+        name="hand_over",
+    )(v_block, first, share)
     return v_block.T, first, share.T
 
 

time: 119 us -> 109 us (0.916)
  local copies, waits for them, and re-layouts: 6.44 us -> 0.85 us
  Pallas kernels: 110 us -> 106 us
    pallas_call x1, Pallas kernels: 110 us -> 103 us  [body(): pl.pallas_call(kernel, out_shape=(jax.ShapeDtypeStruct((COLS, ROWS), BF),...]
    unnamed x9 -> x2, local copies, waits for them, and re-layouts: 6.29 us -> 0.69 us
    pallas_call x0 -> x1, Pallas kernels: none -> 3.7 us  [body(): pl.pallas_call(hand_over, out_shape=(jax.ShapeDtypeStruct((COLS, ROWS), B...]
where the time goes in v3:
time: 109 us
  Pallas kernels  106 us (97%)
  other arithmetic  1.4 us (1%)
    pallas_call x1, Pallas kernels, body(): pl.pallas_call(kernel, out_shape=(jax.ShapeDtypeStruct((COLS, ROWS), BF),...  103 us
    pallas_call x1, Pallas kernels, body(): pl.pallas_call(hand_over, out_shape=(jax.ShapeDtypeStruct((COLS, ROWS), B...  3.7 us

profile of v3, /device:TPU:1, one launch (start us, length us, event | category | flops | bytes accessed | tf_op | source)
XLA Modules:
  0.0 109.2 jit_solution(14544664392935826966)
XLA Ops:
  0.6 0.0 copy-start
  0.7 0.7 copy-done
  1.3 0.1 constant_dynamic-slice_fusion
  1.4 0.1 constant_dynamic-slice_fusion.1
  1.5 1.4 %fusion.4.code_ref = s32[20,40]{1,0:T(8,128)} fusion(s32[40,20]{0,1:T(8,128)} %param.9, s32[20]{0:T(128)S(1)} %get-tuple-element.19, s32[40]{0:T(128)S(1)} %get-tuple-element.16, s32[20]{0:T(128)S(1)} %get-tuple-element.20, s32[40]{0:T(128)S(1)} %get-tuple-element.17, s32[20]{0:T(128)S(1)} %get-tuple-element.18, s32[40]{0:T(128)S(1)} %get-tuple-element.15), kind=kLoop, calls=%fused_computation.9 | loop fusion | flops 16800 | bytes 7120 | tf_op jit(solution)/shard_map/transpose | solution.py:700
  2.9 102.6 %sweeps.1 = (bf16[960,1920]{1,0:T(8,128)(2,1)}, bf16[1920,128]{1,0:T(8,128)(2,1)}, f32[4,1920]{1,0:T(4,128)}) custom-call(s32[20,40]{1,0:T(8,128)} %fusion.4.code_ref, bf16[960,128]{1,0:T(8,128)(2,1)} %bitcast.17, f32[256,1024]{1,0:T(8,128)} %form_hbm.1, f32[20,48]{1,0:T(8,128)} %green_ref.1, bf16[960,128]{1,0:T(8,128)(2,1)} %kmat_ref.1, f32[1920,128]{1,0:T(8,128)} %born_hbm.1), custom_call_target="tpu_custom_call" | custom-call | tf_op jit(solution)/shard_map/sweeps/pallas_call | solution.py:705
  105.5 3.7 %hand_over.1 = (bf16[960,1920]{1,0:T(8,128)(2,1)}, bf16[1920,128]{1,0:T(8,128)(2,1)}, f32[4,1920]{1,0:T(4,128)}) custom-call(bf16[960,1920]{1,0:T(8,128)(2,1)} %get-tuple-element.9.v_in, bf16[1920,128]{1,0:T(8,128)(2,1)} %get-tuple-element.10.f_in, f32[4,1920]{1,0:T(4,128)} %get-tuple-element.11.s_in), custom_call_target="tpu_custom_call" | custom-call | tf_op jit(solution)/shard_map/hand_over/pallas_call | solution.py:752
  (2 shorter events, 0.0 us)
Async XLA Ops:
  0.6 0.7 copy-start

commit v4 on v3

--- a/solution.py
+++ b/solution.py
@@ -116,27 +116,6 @@
             return carry
 
         lax.fori_loop(0, 16, hello, 0)
-
-    for k in range(8):
-        sign[k] = jnp.float32((1.0 - 2.0 * (k // 4)) / (1.0 + k % 4))
-    colp[:, COLS:, :] = jnp.zeros((NROW, 1024 - COLS, LANE), BF)
-    for half in range(2):
-        edge = slice(half * PAD + HROW, (half + 1) * PAD)
-        zsend[edge, :] = jnp.zeros((PAD - HROW, LANE), BF)
-        ssum[edge, :] = jnp.zeros((PAD - HROW, LANE), F32)
-        bornp[edge, :] = jnp.zeros((PAD - HROW, LANE), F32)
-    t32[:, 60:, :] = jnp.zeros((NX * NZ, 4, LANE), F32)
-
-    for b in range(NB):
-        gb_ref[b * MOM:(b + 1) * MOM, :] = jnp.broadcast_to(green_ref[b:b + 1, :], (LANE, MOM)).T
-    weighted[...] = (gb_ref[...] * kmat_ref[...].astype(F32)).astype(BF)
-
-    def spread(i, carry):
-        table[i] = jnp.broadcast_to(form_ref[pl.ds(i, 1), :], (16, GRID)).astype(BF)
-        return carry
-
-    loads[0].wait()
-    lax.fori_loop(0, 128, spread, 0, unroll=4)
 
     n_wait = 7 + 3 + 3 + 1 + 4 + 2
     for from_y in range(NY):
@@ -185,23 +164,52 @@
         ys[k].start()
     colp[row, 0:COLS, :] = rad_ref[...]
 
+    def spread(i, carry):
+        table[i] = jnp.broadcast_to(form_ref[pl.ds(i, 1), :], (16, GRID)).astype(BF)
+        return carry
+
+    loads[0].wait()
+    lax.fori_loop(0, 64, spread, 0, unroll=4)
+
     def s2_copy(xs):
         to_row, to_z = s2_to(xs)
         half = lax.rem(z, 2)
         return copy(mid.at[xs], rowp.at[x, half, to_z], s2_s.at[xs], s2_r.at[half], (to_row, x * NZ + to_z))
 
+    def s2_start(xs):
+        @pl.when(s2_self(xs))
+        def _():
+            rowp[x, lax.rem(z, 2), z] = mid[xs]
+
+        @pl.when(jnp.logical_not(s2_self(xs)))
+        def _():
+            s2_copy(xs).start()
+
+    @pl.when(in_slab)
+    def _():
+        s2_start(x)
+
     for xs in range(2):
         @pl.when(x != xs)
         def _():
             copy(mid.at[xs], mid.at[xs], s1_s.at[0], s1_r.at[xs], sibling).wait_recv()
-
-        @pl.when(s2_self(xs))
-        def _():
-            rowp[x, lax.rem(z, 2), z] = mid[xs]
-
-        @pl.when(jnp.logical_not(s2_self(xs)))
-        def _():
-            s2_copy(xs).start()
+            s2_start(xs)
+
+    for k in range(8):
+        sign[k] = jnp.float32((1.0 - 2.0 * (k // 4)) / (1.0 + k % 4))
+    colp[:, COLS:, :] = jnp.zeros((NROW, 1024 - COLS, LANE), BF)
+    for half in range(2):
+        edge = slice(half * PAD + HROW, (half + 1) * PAD)
+        zsend[edge, :] = jnp.zeros((PAD - HROW, LANE), BF)
+        ssum[edge, :] = jnp.zeros((PAD - HROW, LANE), F32)
+        bornp[edge, :] = jnp.zeros((PAD - HROW, LANE), F32)
+    t32[:, 60:, :] = jnp.zeros((NX * NZ, 4, LANE), F32)
+
+    for b in range(NB):
+        gb_ref[b * MOM:(b + 1) * MOM, :] = jnp.broadcast_to(green_ref[b:b + 1, :], (LANE, MOM)).T
+    weighted[...] = (gb_ref[...] * kmat_ref[...].astype(F32)).astype(BF)
+
+    lax.fori_loop(64, 128, spread, 0, unroll=4)
 
     def flow_at(f):
         if f == 0:
@@ -209,7 +217,7 @@
         return lax.rem(x + f - 1, NX), 1
 
     def steps(f, sign):
-        return 4 if (f <= 2) == (sign > 0) else 3
+        return 4 if (f in (0, 2)) == (sign > 0) else 3
 
     def z_copy(f, sign, s):
         g, half = flow_at(f)
@@ -244,11 +252,15 @@
     def xh2_wait(k):
         xh2(k, 1).wait_recv()
         xh2(k, -1).wait_recv()
-        xh2_forward(k).start()
 
     def xh1(n):
-        ref = rowp.at[lax.rem(x + (3 if n == 2 else 0), NX), 1, z]
+        ref = rowp.at[x, 1, z]
         return copy(ref, ref, x_s.at[24 + n], x_r.at[24 + n], at_x(3 if n == 1 else 1))
+
+    def xf(k):
+        sign = 1 if k % 2 == 0 else -1
+        ref = rowp.at[lax.rem(x + (3 if sign > 0 else 1), NX), 1, piece(k)]
+        return copy(ref, ref, x_s.at[26 + k], x_r.at[26 + k], at_x(1 if sign > 0 else 3))
 
     def flow_start(f):
         z_copy(f, 1, 0).start()
@@ -288,11 +300,16 @@
             if s_ < steps(1, sign_):
                 z_wait(1, sign_, s_)
 
-    def others(s_, *flows):
-        for f in flows:
-            for sign_ in (1, -1):
-                if s_ < steps(f, sign_):
-                    z_wait(f, sign_, s_)
+    def far_step(s_):
+        if s_ < 3:
+            z_wait(4, 1, s_)
+        z_wait(4, -1, s_)
+        if s_ < 3:
+            xf(2 * s_ + 2).start()
+        z_wait(2, 1, s_)
+        xf(2 * s_ + 1).start()
+        if s_ < 3:
+            z_wait(2, -1, s_)
 
     def part_0():
         own_step(0)
@@ -300,7 +317,7 @@
         y_on(5, 11)
         y_on(6, 12)
         xh1(0).wait_recv()
-        xh1(2).start()
+        xf(0).start()
         flow_start(4)
         xh1(1).wait_recv()
         flow_start(2)
@@ -310,9 +327,7 @@
 
     def part_1():
         own_step(1)
-        xh1(2).wait_recv()
-        flow_start(3)
-        others(0, 4, 2)
+        far_step(0)
         xh2_wait(1)
         xh2_wait(2)
 
@@ -326,31 +341,32 @@
 
     def part_3():
         own_step(3)
-        others(1, 4, 2)
-        others(0, 3)
+        far_step(1)
         xh2_wait(5)
         xh2_wait(6)
+        for k in range(7):
+            xh2_forward(k).start()
 
     def before_2():
         xh2_wait(7)
+        xh2_forward(7).start()
 
     def before_3():
-        others(2, 4, 2)
-        others(1, 3)
+        far_step(2)
 
     def before_4():
         for k in range(8):
             xh2_forward(k).wait_recv()
 
     def before_5():
-        z_wait(2, 1, 3)
-        others(2, 3)
+        far_step(3)
 
     def before_6():
-        z_wait(4, -1, 3)
+        pass
 
     def before_7():
-        z_wait(3, -1, 3)
+        for k in range(8):
+            xf(k).wait_recv()
 
     parts_before = {0: part_0, 1: part_1, 2: part_2, 3: part_3}
     befores = {2: before_2, 3: before_3, 4: before_4, 5: before_5, 6: before_6, 7: before_7}
@@ -640,16 +656,18 @@
             s2_copy(xs).wait_send()
     for c in ys:
         c.wait_send()
-    for f in range(5):
-        for sign in (1, -1):
-            for s in range(steps(f, sign)):
-                z_copy(f, sign, s).wait_send()
+    for f in (0, 1, 2, 4):
+        for sign_ in (1, -1):
+            for s in range(steps(f, sign_)):
+                z_copy(f, sign_, s).wait_send()
     for k in range(8):
         xh2(k, 1).wait_send()
         xh2(k, -1).wait_send()
         xh2_forward(k).wait_send()
-    for n in range(3):
+    for n in range(2):
         xh1(n).wait_send()
+    for k in range(8):
+        xf(k).wait_send()
     for n in range(6):
         p_copy(n // 2 + 1, n % 2).wait_send()
     for d in range(1, NZ):
@@ -742,7 +760,7 @@
             pltpu.VMEM((NZ, SH, LANE), F32),
             pltpu.VMEM((NZ, SH, LANE), BF),
             pltpu.VMEM((NZ - 1, SH, LANE), BF),
-            dma((4,)), dma((2,)), dma((2,)), dma((2,)), dma((13,)), dma((13,)), dma((40,)), dma((40,)), dma((27,)), dma((27,)),
+            dma((4,)), dma((2,)), dma((2,)), dma((2,)), dma((13,)), dma((13,)), dma((40,)), dma((40,)), dma((34,)), dma((34,)),
             dma((6,)), dma((6,)), dma((8,)), dma((8,)), dma((4,)), dma((4,)), dma((4,)), dma((16,)), dma((4,)), dma((4,)),
             dma((8,)), dma((8,)), dma((4,)), dma((4,)), dma((4,)), dma((4,)), dma((8,)), dma((8,)), dma((2,)), dma((9,)),
         ],

time: 109 us -> 108 us (level)
    pallas_call x1, Pallas kernels: 103 us -> 101 us  [body(): pl.pallas_call(kernel, out_shape=(jax.ShapeDtypeStruct((COLS, ROWS), BF),...]
where the time goes in v4:
time: 108 us
  Pallas kernels  105 us (97%)
  other arithmetic  1.4 us (1%)
    pallas_call x1, Pallas kernels, body(): pl.pallas_call(kernel, out_shape=(jax.ShapeDtypeStruct((COLS, ROWS), BF),...  101 us
    pallas_call x1, Pallas kernels, body(): pl.pallas_call(hand_over, out_shape=(jax.ShapeDtypeStruct((COLS, ROWS), B...  3.7 us

profile of v4, /device:TPU:1, one launch (start us, length us, event | category | flops | bytes accessed | tf_op | source)
XLA Modules:
  0.0 108.0 jit_solution(17039628040017852886)
XLA Ops:
  0.6 0.0 copy-start
  0.7 0.7 copy-done
  1.3 0.1 constant_dynamic-slice_fusion
  1.4 0.1 constant_dynamic-slice_fusion.1
  1.5 1.4 %fusion.4.code_ref = s32[20,40]{1,0:T(8,128)} fusion(s32[40,20]{0,1:T(8,128)} %param.9, s32[20]{0:T(128)S(1)} %get-tuple-element.19, s32[40]{0:T(128)S(1)} %get-tuple-element.16, s32[20]{0:T(128)S(1)} %get-tuple-element.20, s32[40]{0:T(128)S(1)} %get-tuple-element.17, s32[20]{0:T(128)S(1)} %get-tuple-element.18, s32[40]{0:T(128)S(1)} %get-tuple-element.15), kind=kLoop, calls=%fused_computation.9 | loop fusion | flops 16800 | bytes 7120 | tf_op jit(solution)/shard_map/transpose | solution.py:718
  2.9 101.4 %sweeps.1 = (bf16[960,1920]{1,0:T(8,128)(2,1)}, bf16[1920,128]{1,0:T(8,128)(2,1)}, f32[4,1920]{1,0:T(4,128)}) custom-call(s32[20,40]{1,0:T(8,128)} %fusion.4.code_ref, bf16[960,128]{1,0:T(8,128)(2,1)} %bitcast.17, f32[256,1024]{1,0:T(8,128)} %form_hbm.1, f32[20,48]{1,0:T(8,128)} %green_ref.1, bf16[960,128]{1,0:T(8,128)(2,1)} %kmat_ref.1, f32[1920,128]{1,0:T(8,128)} %born_hbm.1), custom_call_target="tpu_custom_call" | custom-call | tf_op jit(solution)/shard_map/sweeps/pallas_call | solution.py:723
  104.3 3.7 %hand_over.1 = (bf16[960,1920]{1,0:T(8,128)(2,1)}, bf16[1920,128]{1,0:T(8,128)(2,1)}, f32[4,1920]{1,0:T(4,128)}) custom-call(bf16[960,1920]{1,0:T(8,128)(2,1)} %get-tuple-element.9.v_in, bf16[1920,128]{1,0:T(8,128)(2,1)} %get-tuple-element.10.f_in, f32[4,1920]{1,0:T(4,128)} %get-tuple-element.11.s_in), custom_call_target="tpu_custom_call" | custom-call | tf_op jit(solution)/shard_map/hand_over/pallas_call | solution.py:770
  (2 shorter events, 0.0 us)
Async XLA Ops:
  0.6 0.7 copy-start

commit v5 on v4

--- a/solution.py
+++ b/solution.py
@@ -335,6 +335,8 @@
         own_step(2)
         xh2_wait(3)
         xh2_wait(4)
+        for k in range(3):
+            xh2_forward(k).start()
         loads[1].wait()
         for half in range(2):
             bornp[half * PAD:half * PAD + HROW, :] = born_ref[pl.ds(pl.multiple_of(half * COLS + x * HROW, HROW), HROW), :]
@@ -344,7 +346,7 @@
         far_step(1)
         xh2_wait(5)
         xh2_wait(6)
-        for k in range(7):
+        for k in range(3, 7):
             xh2_forward(k).start()
 
     def before_2():

time: 108 us -> 109 us (level)
  no operation moved by 1% of the time
where the time goes in v5:
time: 109 us
  Pallas kernels  106 us (97%)
  other arithmetic  1.4 us (1%)
    pallas_call x1, Pallas kernels, body(): pl.pallas_call(kernel, out_shape=(jax.ShapeDtypeStruct((COLS, ROWS), BF),...  102 us
    pallas_call x1, Pallas kernels, body(): pl.pallas_call(hand_over, out_shape=(jax.ShapeDtypeStruct((COLS, ROWS), B...  3.7 us

profile of v5, /device:TPU:1, one launch (start us, length us, event | category | flops | bytes accessed | tf_op | source)
XLA Modules:
  0.0 108.8 jit_solution(1528348203991343153)
XLA Ops:
  0.6 0.0 copy-start
  0.7 0.7 copy-done
  1.3 0.1 constant_dynamic-slice_fusion
  1.4 0.1 constant_dynamic-slice_fusion.1
  1.5 1.4 %fusion.4.code_ref = s32[20,40]{1,0:T(8,128)} fusion(s32[40,20]{0,1:T(8,128)} %param.9, s32[20]{0:T(128)S(1)} %get-tuple-element.19, s32[40]{0:T(128)S(1)} %get-tuple-element.16, s32[20]{0:T(128)S(1)} %get-tuple-element.20, s32[40]{0:T(128)S(1)} %get-tuple-element.17, s32[20]{0:T(128)S(1)} %get-tuple-element.18, s32[40]{0:T(128)S(1)} %get-tuple-element.15), kind=kLoop, calls=%fused_computation.9 | loop fusion | flops 16800 | bytes 7120 | tf_op jit(solution)/shard_map/transpose | solution.py:720
  2.9 102.2 %sweeps.1 = (bf16[960,1920]{1,0:T(8,128)(2,1)}, bf16[1920,128]{1,0:T(8,128)(2,1)}, f32[4,1920]{1,0:T(4,128)}) custom-call(s32[20,40]{1,0:T(8,128)} %fusion.4.code_ref, bf16[960,128]{1,0:T(8,128)(2,1)} %bitcast.17, f32[256,1024]{1,0:T(8,128)} %form_hbm.1, f32[20,48]{1,0:T(8,128)} %green_ref.1, bf16[960,128]{1,0:T(8,128)(2,1)} %kmat_ref.1, f32[1920,128]{1,0:T(8,128)} %born_hbm.1), custom_call_target="tpu_custom_call" | custom-call | tf_op jit(solution)/shard_map/sweeps/pallas_call | solution.py:725
  105.1 3.7 %hand_over.1 = (bf16[960,1920]{1,0:T(8,128)(2,1)}, bf16[1920,128]{1,0:T(8,128)(2,1)}, f32[4,1920]{1,0:T(4,128)}) custom-call(bf16[960,1920]{1,0:T(8,128)(2,1)} %get-tuple-element.9.v_in, bf16[1920,128]{1,0:T(8,128)(2,1)} %get-tuple-element.10.f_in, f32[4,1920]{1,0:T(4,128)} %get-tuple-element.11.s_in), custom_call_target="tpu_custom_call" | custom-call | tf_op jit(solution)/shard_map/hand_over/pallas_call | solution.py:772
  (2 shorter events, 0.0 us)
Async XLA Ops:
  0.6 0.7 copy-start
